TPU v7x, 512 devices: a whole 4x8x8 slice. The times are simulated.
512 devices in a mesh: pix: 512 (over x, z, y, core).
Axes of the slice: x: 4, y: 8, z: 8, core: 2. Of those that a mesh axis runs over, the one named last changes fastest.
Arguments:
- input_maps: bfloat16 [64, 131072], P(None, 'pix'), may hold values from -6 to 6
- cheb_weights: bfloat16 [5, 64, 64], replicated, may hold values from -0.3125 to 0.3125
- cotangent: bfloat16 [64, 131072], P(None, 'pix'), may hold values from -6 to 6
- neighbours: int32 [9, 131072], P(None, 'pix'), may hold values from 0 to 767, as said below
- lap_weights: float32 [9, 131072], P(None, 'pix'), may hold values from -0.25 to 0.25
- send_rows: int32 [4096, 64], P('pix'), may hold values from 0 to 256, as said below
Outputs:
- output_maps: bfloat16 [64, 131072], P(None, 'pix')
- map_gradient: bfloat16 [64, 131072], P(None, 'pix')
- weight_gradient: float32 [5, 64, 64], replicated
Inputs may be any that keep to these rules, and one draw needn't show every extreme that they name: `send_rows`: with offset_o = 1, -1, 16, -16, 17, 15, 1 - 16, -1 - 16: row 8 * d + o lists pixels of device d (numbered 0 to 255 within the device) that device (d + offset_o) mod 512 reads. Its live entries come first and are distinct; there are 32 to 64 of them, and for each o some device's list is full. The other entries equal 256. neighbours[0, p] is p's own column of extended_d. Every other entry is a column of the device's own pixels or a received column whose list entry is live. Each live received column 256 + o * 64 + j is read by exactly one pixel of the device, in entry 1 + o.
All inputs are finite; a program needn't handle non-finite values.
Results may differ from a plain program's by a relative error of at most 0.0046.
Values sent between devices are 32-bit elements; how exact they have to be, the bound alone decides.
A program may use at most 64 MiB of HBM per device.

v0:
```python
import math

import jax
import jax.numpy as jnp
from jax import lax
from jax.sharding import PartitionSpec as P

COUT = 64
KTERMS = 5
HALO = 64
TILE_ROW = 16
PEERS = 8
STENCIL = 9


row_moves = [1, -1, 0, 0, 1, -1, 1, -1]
column_moves = [0, 0, 1, -1, 1, 1, -1, -1]


def shifted(value, axis, by):
    length = lax.axis_size(axis)
    return lax.ppermute(value, axis, [(i, (i + by) % length) for i in range(length)])


def trade(pieces, direction):
    return [
        shifted(
            pieces[peer_index],
            "pix",
            direction * (row_moves[peer_index] + column_moves[peer_index] * TILE_ROW),
        )
        for peer_index in range(PEERS)
    ]


def local(input_maps, cheb_weights, cotangent, neighbours, lap_weights, send_rows):
    channels = input_maps.shape[0]
    pixels = input_maps.shape[1]
    ext_width = pixels + PEERS * HALO
    flat_sends = send_rows.reshape(-1)

    def forward_pieces(values):
        padded = jnp.concatenate([values, jnp.zeros((channels, 1), jnp.float32)], axis=1)
        listed = padded[:, flat_sends]
        return [
            listed[:, peer_index * HALO : (peer_index + 1) * HALO] for peer_index in range(PEERS)
        ]

    def adjoint_pieces(values):
        spread = jnp.zeros((channels, ext_width), jnp.float32)
        for stencil_slot in range(STENCIL):
            spread = spread.at[:, neighbours[stencil_slot]].add(
                lap_weights[stencil_slot][None, :] * values
            )
        pieces = [
            spread[:, pixels + peer_index * HALO : pixels + (peer_index + 1) * HALO]
            for peer_index in range(PEERS)
        ]
        return (spread, pieces)

    flat_weights = cheb_weights.reshape(KTERMS * channels, COUT)
    adjoints = jnp.dot(flat_weights, cotangent, preferred_element_type=jnp.float32).reshape(
        KTERMS, channels, pixels
    )
    adjoint_list = [adjoints[term_index] for term_index in range(KTERMS)]

    def adjoint_update(applied, carried):
        if applied >= 2:
            adjoint_list[applied - 1] = adjoint_list[applied - 1] + 2.0 * carried
            adjoint_list[applied - 2] = adjoint_list[applied - 2] - adjoint_list[applied]
        else:
            adjoint_list[0] = adjoint_list[0] + carried

    rounded_terms = []
    terms = []
    for term_index in range(KTERMS):
        if term_index == 0:
            new_term = input_maps.astype(jnp.float32)
        else:
            previous = terms[-1]
            outgoing = forward_pieces(previous)
            received = trade(outgoing, 1)
            extended = jnp.concatenate([previous] + list(received), axis=1)
            summed = lap_weights[0][None, :] * extended[:, neighbours[0]]
            for forward_stencil_slot in range(1, STENCIL):
                summed = (
                    summed
                    + lap_weights[forward_stencil_slot][None, :]
                    * extended[:, neighbours[forward_stencil_slot]]
                )
            if term_index == 1:
                new_term = summed
            else:
                new_term = 2.0 * summed - terms[-2]
        terms.append(new_term)
        rounded = new_term.astype(jnp.bfloat16)
        rounded_terms.append(rounded)
    stacked = jnp.concatenate(rounded_terms, axis=0)
    output_sum = jnp.einsum("kf,kp->fp", flat_weights, stacked, preferred_element_type=jnp.float32)
    local_grad = jnp.einsum(
        "kp,fp->kf", stacked, cotangent, preferred_element_type=jnp.float32
    ).reshape(KTERMS, channels, COUT)
    output_maps = output_sum.astype(jnp.bfloat16)
    total_pixels = lax.axis_size("pix") * pixels
    weight_gradient = lax.psum(local_grad, "pix") / math.sqrt(total_pixels)
    for applied in range(KTERMS - 1, 0, -1):
        spread, back_pieces = adjoint_pieces(adjoint_list[applied])
        returned = trade(back_pieces, -1)
        own_part = jnp.concatenate(
            [spread[:, :pixels], jnp.zeros((channels, 1), jnp.float32)], axis=1
        )
        own_part = own_part.at[:, flat_sends].add(jnp.concatenate(returned, axis=1))
        adjoint_update(applied, own_part[:, :pixels])
    map_gradient = adjoint_list[0].astype(jnp.bfloat16)
    return (output_maps, map_gradient, weight_gradient)


def solution(mesh):
    return jax.shard_map(
        local,
        mesh=mesh,
        in_specs=(
            P(None, "pix"),
            P(),
            P(None, "pix"),
            P(None, "pix"),
            P(None, "pix"),
            P("pix", None),
        ),
        out_specs=(P(None, "pix"), P(None, "pix"), P()),
        check_vma=False,
    )
```

profile of v0, /device:TPU:1, one launch (start us, length us, event | category | flops | bytes accessed | tf_op | source)
XLA Modules:
  0.0 717.8 jit_solution(6406805491205012385)
XLA Ops:
  29.4 8.8 %collective-permute-start.32 = (f32[64,64]{0,1:T(8,128)S(1)}, f32[64,64]{0,1:T(8,128)S(1)}, u32[]{:S(2)}, u32[]{:S(2)}) collective-permute-start(f32[64,64]{0,1:T(8,128)S(1)} %get-tuple-element.46), channel_id=1, source_target_pairs={{0,511},{1,0},{2,1},{3,2},{4,3},{5,4},{6,5},{7,6},{8,7},{9,8},{10,... | collective-permute-start | bytes 49160 | tf_op jit(solution)/shard_map/ppermute | solution.py:22
  40.1 8.7 %collective-permute-start.34 = (f32[64,64]{0,1:T(8,128)S(1)}, f32[64,64]{0,1:T(8,128)S(1)}, u32[]{:S(2)}, u32[]{:S(2)}) collective-permute-start(f32[64,64]{0,1:T(8,128)S(1)} %get-tuple-element.44), channel_id=1, source_target_pairs={{0,496},{1,497},{2,498},{3,499},{4,500},{5,501},{6,502},{7,503},{8... | collective-permute-start | bytes 49160 | tf_op jit(solution)/shard_map/ppermute | solution.py:22
  50.7 9.1 %collective-permute-start.36 = (f32[64,64]{0,1:T(8,128)S(1)}, f32[64,64]{0,1:T(8,128)S(1)}, u32[]{:S(2)}, u32[]{:S(2)}) collective-permute-start(f32[64,64]{0,1:T(8,128)S(1)} %get-tuple-element.42), channel_id=1, source_target_pairs={{0,495},{1,496},{2,497},{3,498},{4,499},{5,500},{6,501},{7,502},{8... | collective-permute-start | bytes 49160 | tf_op jit(solution)/shard_map/ppermute | solution.py:22
  64.7 9.4 %collective-permute-start.38 = (f32[64,64]{0,1:T(8,128)S(1)}, f32[64,64]{0,1:T(8,128)S(1)}, u32[]{:S(2)}, u32[]{:S(2)}) collective-permute-start(f32[64,64]{0,1:T(8,128)S(1)} %get-tuple-element.40), channel_id=1, source_target_pairs={{0,15},{1,16},{2,17},{3,18},{4,19},{5,20},{6,21},{7,22},{8,23},{9,... | collective-permute-start | bytes 49160 | tf_op jit(solution)/shard_map/ppermute | solution.py:22
  80.5 4.5 collective-permute-start.2
  85.0 4.1 collective-permute-start.3
  114.4 8.2 %collective-permute-start.5 = (f32[64,64]{1,0:T(8,128)S(1)}, f32[64,64]{1,0:T(8,128)S(1)}, u32[]{:S(2)}, u32[]{:S(2)}) collective-permute-start(f32[64,64]{1,0:T(8,128)S(1)} %get-tuple-element.82), channel_id=1, source_target_pairs={{0,15},{1,16},{2,17},{3,18},{4,19},{5,20},{6,21},{7,22},{8,23},{9,... | collective-permute-start | bytes 49160 | tf_op jit(solution)/shard_map/ppermute | solution.py:22
  124.6 9.0 %collective-permute-start.7 = (f32[64,64]{1,0:T(8,128)S(1)}, f32[64,64]{1,0:T(8,128)S(1)}, u32[]{:S(2)}, u32[]{:S(2)}) collective-permute-start(f32[64,64]{1,0:T(8,128)S(1)} %get-tuple-element.80), channel_id=1, source_target_pairs={{0,495},{1,496},{2,497},{3,498},{4,499},{5,500},{6,501},{7,502},{8... | collective-permute-start | bytes 49160 | tf_op jit(solution)/shard_map/ppermute | solution.py:22
  133.7 9.5 %collective-permute-start.40 = (f32[64,64]{0,1:T(8,128)S(1)}, f32[64,64]{0,1:T(8,128)S(1)}, u32[]{:S(2)}, u32[]{:S(2)}) collective-permute-start(f32[64,64]{0,1:T(8,128)S(1)} %get-tuple-element.38), channel_id=1, source_target_pairs={{0,511},{1,0},{2,1},{3,2},{4,3},{5,4},{6,5},{7,6},{8,7},{9,8},{10,... | collective-permute-start | bytes 49160 | tf_op jit(solution)/shard_map/ppermute | solution.py:22
  150.4 6.0 collective-permute-start.44
  167.5 9.4 %collective-permute-start.46 = (f32[64,64]{0,1:T(8,128)S(1)}, f32[64,64]{0,1:T(8,128)S(1)}, u32[]{:S(2)}, u32[]{:S(2)}) collective-permute-start(f32[64,64]{0,1:T(8,128)S(1)} %get-tuple-element.32), channel_id=1, source_target_pairs={{0,15},{1,16},{2,17},{3,18},{4,19},{5,20},{6,21},{7,22},{8,23},{9,... | collective-permute-start | bytes 49160 | tf_op jit(solution)/shard_map/ppermute | solution.py:22
  180.9 6.7 collective-permute-start.11
  191.7 7.7 %collective-permute-start.14 = (f32[64,64]{1,0:T(8,128)S(1)}, f32[64,64]{1,0:T(8,128)S(1)}, u32[]{:S(2)}, u32[]{:S(2)}) collective-permute-start(f32[64,64]{1,0:T(8,128)S(1)} %get-tuple-element.73), channel_id=1, source_target_pairs={{0,497},{1,498},{2,499},{3,500},{4,501},{5,502},{6,503},{7,504},{8... | collective-permute-start | bytes 49160 | tf_op jit(solution)/shard_map/ppermute | solution.py:22
  227.8 6.3 collective-permute-start.9
  241.8 9.8 %collective-permute-start.48 = (f32[64,64]{0,1:T(8,128)S(1)}, f32[64,64]{0,1:T(8,128)S(1)}, u32[]{:S(2)}, u32[]{:S(2)}) collective-permute-start(f32[64,64]{0,1:T(8,128)S(1)} %get-tuple-element.30), channel_id=1, source_target_pairs={{0,511},{1,0},{2,1},{3,2},{4,3},{5,4},{6,5},{7,6},{8,7},{9,8},{10,... | collective-permute-start | bytes 49160 | tf_op jit(solution)/shard_map/ppermute | solution.py:22
  258.8 12.8 %collective-permute-start.52 = (f32[64,64]{0,1:T(8,128)S(1)}, f32[64,64]{0,1:T(8,128)S(1)}, u32[]{:S(2)}, u32[]{:S(2)}) collective-permute-start(f32[64,64]{0,1:T(8,128)S(1)} %get-tuple-element.26), channel_id=1, source_target_pairs={{0,495},{1,496},{2,497},{3,498},{4,499},{5,500},{6,501},{7,502},{8... | collective-permute-start | bytes 49160 | tf_op jit(solution)/shard_map/ppermute | solution.py:22
  275.8 10.0 %collective-permute-start.54 = (f32[64,64]{0,1:T(8,128)S(1)}, f32[64,64]{0,1:T(8,128)S(1)}, u32[]{:S(2)}, u32[]{:S(2)}) collective-permute-start(f32[64,64]{0,1:T(8,128)S(1)} %get-tuple-element.24), channel_id=1, source_target_pairs={{0,15},{1,16},{2,17},{3,18},{4,19},{5,20},{6,21},{7,22},{8,23},{9,... | collective-permute-start | bytes 49160 | tf_op jit(solution)/shard_map/ppermute | solution.py:22
  290.2 4.5 collective-permute-start.18
  294.7 4.1 collective-permute-start.19
  302.7 5.4 collective-permute-start.21
  308.2 4.3 collective-permute-start.22
  312.5 6.6 collective-permute-start.23
  342.4 6.9 collective-permute-start.25
  368.5 6.7 collective-permute-start.27
  377.1 5.9 collective-permute-start.29
  383.1 3.9 collective-permute-start.30
  387.0 7.1 collective-permute-start.31
  394.2 9.5 %collective-permute-start.56 = (f32[64,64]{0,1:T(8,128)S(1)}, f32[64,64]{0,1:T(8,128)S(1)}, u32[]{:S(2)}, u32[]{:S(2)}) collective-permute-start(f32[64,64]{0,1:T(8,128)S(1)} %get-tuple-element.22), channel_id=1, source_target_pairs={{0,511},{1,0},{2,1},{3,2},{4,3},{5,4},{6,5},{7,6},{8,7},{9,8},{10,... | collective-permute-start | bytes 49160 | tf_op jit(solution)/shard_map/ppermute | solution.py:22
  411.0 6.0 collective-permute-start.60
  430.2 9.4 %collective-permute-start.62 = (f32[64,64]{0,1:T(8,128)S(1)}, f32[64,64]{0,1:T(8,128)S(1)}, u32[]{:S(2)}, u32[]{:S(2)}) collective-permute-start(f32[64,64]{0,1:T(8,128)S(1)} %get-tuple-element.16), channel_id=1, source_target_pairs={{0,15},{1,16},{2,17},{3,18},{4,19},{5,20},{6,21},{7,22},{8,23},{9,... | collective-permute-start | bytes 49160 | tf_op jit(solution)/shard_map/ppermute | solution.py:22
  441.7 6.8 collective-permute-done.63
  452.8 256.1 %all-reduce.6.cloned.1.call-done = f32[5,64,64]{2,1,0:T(8,128)} async-done(((f32[5,64,64]{2,1,0:T(8,128)}), f32[5,64,64]{2,1,0:T(8,128)}) %all-reduce.6.cloned.1.call-update) | async-done | bytes 81936 | tf_op jit(solution)/shard_map/psum | solution.py:105
  (460 shorter events, 217.0 us)
Async XLA Ops:
  7.2 701.7 %all-reduce.6.cloned.1.call-start = ((), (), s32[]{:S(2)}) async-start(), calls=%async_computation | async-start | bytes 327680 | tf_op jit(solution)/shard_map/psum | solution.py:105
  29.4 33.4 %collective-permute-start.32 = (f32[64,64]{0,1:T(8,128)S(1)}, f32[64,64]{0,1:T(8,128)S(1)}, u32[]{:S(2)}, u32[]{:S(2)}) collective-permute-start(f32[64,64]{0,1:T(8,128)S(1)} %get-tuple-element.46), channel_id=1, source_target_pairs={{0,511},{1,0},{2,1},{3,2},{4,3},{5,4},{6,5},{7,6},{8,7},{9,8},{10,... | collective-permute-start | bytes 49160 | tf_op jit(solution)/shard_map/ppermute | solution.py:22
  40.1 34.1 %collective-permute-start.34 = (f32[64,64]{0,1:T(8,128)S(1)}, f32[64,64]{0,1:T(8,128)S(1)}, u32[]{:S(2)}, u32[]{:S(2)}) collective-permute-start(f32[64,64]{0,1:T(8,128)S(1)} %get-tuple-element.44), channel_id=1, source_target_pairs={{0,496},{1,497},{2,498},{3,499},{4,500},{5,501},{6,502},{7,503},{8... | collective-permute-start | bytes 49160 | tf_op jit(solution)/shard_map/ppermute | solution.py:22
  76.1 38.3 %collective-permute-start = (f32[64,64]{1,0:T(8,128)S(1)}, f32[64,64]{1,0:T(8,128)S(1)}, u32[]{:S(2)}, u32[]{:S(2)}) collective-permute-start(f32[64,64]{1,0:T(8,128)S(1)} %get-tuple-element.87), channel_id=1, source_target_pairs={{0,1},{1,2},{2,3},{3,4},{4,5},{5,6},{6,7},{7,8},{8,9},{9,10},{10,1... | collective-permute-start | bytes 49160 | tf_op jit(solution)/shard_map/ppermute | solution.py:22
  78.1 44.6 %collective-permute-start.1 = (f32[64,64]{1,0:T(8,128)S(1)}, f32[64,64]{1,0:T(8,128)S(1)}, u32[]{:S(2)}, u32[]{:S(2)}) collective-permute-start(f32[64,64]{1,0:T(8,128)S(1)} %get-tuple-element.86), channel_id=1, source_target_pairs={{0,511},{1,0},{2,1},{3,2},{4,3},{5,4},{6,5},{7,6},{8,7},{9,8},{10,... | collective-permute-start | bytes 49160 | tf_op jit(solution)/shard_map/ppermute | solution.py:22
  80.5 44.1 %collective-permute-start.2 = (f32[64,64]{1,0:T(8,128)S(1)}, f32[64,64]{1,0:T(8,128)S(1)}, u32[]{:S(2)}, u32[]{:S(2)}) collective-permute-start(f32[64,64]{1,0:T(8,128)S(1)} %get-tuple-element.85), channel_id=1, source_target_pairs={{0,16},{1,17},{2,18},{3,19},{4,20},{5,21},{6,22},{7,23},{8,24},{9,... | collective-permute-start | bytes 49160 | tf_op jit(solution)/shard_map/ppermute | solution.py:22
  85.0 48.6 %collective-permute-start.3 = (f32[64,64]{1,0:T(8,128)S(1)}, f32[64,64]{1,0:T(8,128)S(1)}, u32[]{:S(2)}, u32[]{:S(2)}) collective-permute-start(f32[64,64]{1,0:T(8,128)S(1)} %get-tuple-element.84), channel_id=1, source_target_pairs={{0,496},{1,497},{2,498},{3,499},{4,500},{5,501},{6,502},{7,503},{8... | collective-permute-start | bytes 49160 | tf_op jit(solution)/shard_map/ppermute | solution.py:22
  89.2 54.0 %collective-permute-start.4 = (f32[64,64]{1,0:T(8,128)S(1)}, f32[64,64]{1,0:T(8,128)S(1)}, u32[]{:S(2)}, u32[]{:S(2)}) collective-permute-start(f32[64,64]{1,0:T(8,128)S(1)} %get-tuple-element.83), channel_id=1, source_target_pairs={{0,17},{1,18},{2,19},{3,20},{4,21},{5,22},{6,23},{7,24},{8,25},{9,... | collective-permute-start | bytes 49160 | tf_op jit(solution)/shard_map/ppermute | solution.py:22
  114.4 30.7 %collective-permute-start.5 = (f32[64,64]{1,0:T(8,128)S(1)}, f32[64,64]{1,0:T(8,128)S(1)}, u32[]{:S(2)}, u32[]{:S(2)}) collective-permute-start(f32[64,64]{1,0:T(8,128)S(1)} %get-tuple-element.82), channel_id=1, source_target_pairs={{0,15},{1,16},{2,17},{3,18},{4,19},{5,20},{6,21},{7,22},{8,23},{9,... | collective-permute-start | bytes 49160 | tf_op jit(solution)/shard_map/ppermute | solution.py:22
  133.7 31.9 %collective-permute-start.40 = (f32[64,64]{0,1:T(8,128)S(1)}, f32[64,64]{0,1:T(8,128)S(1)}, u32[]{:S(2)}, u32[]{:S(2)}) collective-permute-start(f32[64,64]{0,1:T(8,128)S(1)} %get-tuple-element.38), channel_id=1, source_target_pairs={{0,511},{1,0},{2,1},{3,2},{4,3},{5,4},{6,5},{7,6},{8,7},{9,8},{10,... | collective-permute-start | bytes 49160 | tf_op jit(solution)/shard_map/ppermute | solution.py:22
  145.1 31.9 %collective-permute-start.42 = (f32[64,64]{0,1:T(8,128)S(1)}, f32[64,64]{0,1:T(8,128)S(1)}, u32[]{:S(2)}, u32[]{:S(2)}) collective-permute-start(f32[64,64]{0,1:T(8,128)S(1)} %get-tuple-element.36), channel_id=1, source_target_pairs={{0,496},{1,497},{2,498},{3,499},{4,500},{5,501},{6,502},{7,503},{8... | collective-permute-start | bytes 49160 | tf_op jit(solution)/shard_map/ppermute | solution.py:22
  147.0 31.9 %collective-permute-start.43 = (f32[64,64]{0,1:T(8,128)S(1)}, f32[64,64]{0,1:T(8,128)S(1)}, u32[]{:S(2)}, u32[]{:S(2)}) collective-permute-start(f32[64,64]{0,1:T(8,128)S(1)} %get-tuple-element.35), channel_id=1, source_target_pairs={{0,16},{1,17},{2,18},{3,19},{4,20},{5,21},{6,22},{7,23},{8,24},{9,... | collective-permute-start | bytes 49160 | tf_op jit(solution)/shard_map/ppermute | solution.py:22
  150.4 30.5 %collective-permute-start.44 = (f32[64,64]{0,1:T(8,128)S(1)}, f32[64,64]{0,1:T(8,128)S(1)}, u32[]{:S(2)}, u32[]{:S(2)}) collective-permute-start(f32[64,64]{0,1:T(8,128)S(1)} %get-tuple-element.34), channel_id=1, source_target_pairs={{0,495},{1,496},{2,497},{3,498},{4,499},{5,500},{6,501},{7,502},{8... | collective-permute-start | bytes 49160 | tf_op jit(solution)/shard_map/ppermute | solution.py:22
  178.9 43.6 %collective-permute-start.10 = (f32[64,64]{1,0:T(8,128)S(1)}, f32[64,64]{1,0:T(8,128)S(1)}, u32[]{:S(2)}, u32[]{:S(2)}) collective-permute-start(f32[64,64]{1,0:T(8,128)S(1)} %get-tuple-element.77), channel_id=1, source_target_pairs={{0,16},{1,17},{2,18},{3,19},{4,20},{5,21},{6,22},{7,23},{8,24},{9,... | collective-permute-start | bytes 49160 | tf_op jit(solution)/shard_map/ppermute | solution.py:22
  180.9 44.9 %collective-permute-start.11 = (f32[64,64]{1,0:T(8,128)S(1)}, f32[64,64]{1,0:T(8,128)S(1)}, u32[]{:S(2)}, u32[]{:S(2)}) collective-permute-start(f32[64,64]{1,0:T(8,128)S(1)} %get-tuple-element.76), channel_id=1, source_target_pairs={{0,496},{1,497},{2,498},{3,499},{4,500},{5,501},{6,502},{7,503},{8... | collective-permute-start | bytes 49160 | tf_op jit(solution)/shard_map/ppermute | solution.py:22
  187.6 40.2 %collective-permute-start.12 = (f32[64,64]{1,0:T(8,128)S(1)}, f32[64,64]{1,0:T(8,128)S(1)}, u32[]{:S(2)}, u32[]{:S(2)}) collective-permute-start(f32[64,64]{1,0:T(8,128)S(1)} %get-tuple-element.75), channel_id=1, source_target_pairs={{0,17},{1,18},{2,19},{3,20},{4,21},{5,22},{6,23},{7,24},{8,25},{9,... | collective-permute-start | bytes 49160 | tf_op jit(solution)/shard_map/ppermute | solution.py:22
  189.6 44.6 %collective-permute-start.13 = (f32[64,64]{1,0:T(8,128)S(1)}, f32[64,64]{1,0:T(8,128)S(1)}, u32[]{:S(2)}, u32[]{:S(2)}) collective-permute-start(f32[64,64]{1,0:T(8,128)S(1)} %get-tuple-element.74), channel_id=1, source_target_pairs={{0,15},{1,16},{2,17},{3,18},{4,19},{5,20},{6,21},{7,22},{8,23},{9,... | collective-permute-start | bytes 49160 | tf_op jit(solution)/shard_map/ppermute | solution.py:22
  191.7 42.5 %collective-permute-start.14 = (f32[64,64]{1,0:T(8,128)S(1)}, f32[64,64]{1,0:T(8,128)S(1)}, u32[]{:S(2)}, u32[]{:S(2)}) collective-permute-start(f32[64,64]{1,0:T(8,128)S(1)} %get-tuple-element.73), channel_id=1, source_target_pairs={{0,497},{1,498},{2,499},{3,500},{4,501},{5,502},{6,503},{7,504},{8... | collective-permute-start | bytes 49160 | tf_op jit(solution)/shard_map/ppermute | solution.py:22
  241.8 32.1 %collective-permute-start.48 = (f32[64,64]{0,1:T(8,128)S(1)}, f32[64,64]{0,1:T(8,128)S(1)}, u32[]{:S(2)}, u32[]{:S(2)}) collective-permute-start(f32[64,64]{0,1:T(8,128)S(1)} %get-tuple-element.30), channel_id=1, source_target_pairs={{0,511},{1,0},{2,1},{3,2},{4,3},{5,4},{6,5},{7,6},{8,7},{9,8},{10,... | collective-permute-start | bytes 49160 | tf_op jit(solution)/shard_map/ppermute | solution.py:22
  253.5 32.3 %collective-permute-start.50 = (f32[64,64]{0,1:T(8,128)S(1)}, f32[64,64]{0,1:T(8,128)S(1)}, u32[]{:S(2)}, u32[]{:S(2)}) collective-permute-start(f32[64,64]{0,1:T(8,128)S(1)} %get-tuple-element.28), channel_id=1, source_target_pairs={{0,496},{1,497},{2,498},{3,499},{4,500},{5,501},{6,502},{7,503},{8... | collective-permute-start | bytes 49160 | tf_op jit(solution)/shard_map/ppermute | solution.py:22
  255.4 32.3 %collective-permute-start.51 = (f32[64,64]{0,1:T(8,128)S(1)}, f32[64,64]{0,1:T(8,128)S(1)}, u32[]{:S(2)}, u32[]{:S(2)}) collective-permute-start(f32[64,64]{0,1:T(8,128)S(1)} %get-tuple-element.27), channel_id=1, source_target_pairs={{0,16},{1,17},{2,18},{3,19},{4,20},{5,21},{6,22},{7,23},{8,24},{9,... | collective-permute-start | bytes 49160 | tf_op jit(solution)/shard_map/ppermute | solution.py:22
  258.8 31.4 %collective-permute-start.52 = (f32[64,64]{0,1:T(8,128)S(1)}, f32[64,64]{0,1:T(8,128)S(1)}, u32[]{:S(2)}, u32[]{:S(2)}) collective-permute-start(f32[64,64]{0,1:T(8,128)S(1)} %get-tuple-element.26), channel_id=1, source_target_pairs={{0,495},{1,496},{2,497},{3,498},{4,499},{5,500},{6,501},{7,502},{8... | collective-permute-start | bytes 49160 | tf_op jit(solution)/shard_map/ppermute | solution.py:22
  298.9 28.9 %collective-permute-start.55 = (f32[64,64]{0,1:T(8,128)S(1)}, f32[64,64]{0,1:T(8,128)S(1)}, u32[]{:S(2)}, u32[]{:S(2)}) collective-permute-start(f32[64,64]{0,1:T(8,128)S(1)} %get-tuple-element.23), channel_id=1, source_target_pairs={{0,17},{1,18},{2,19},{3,20},{4,21},{5,22},{6,23},{7,24},{8,25},{9,... | collective-permute-start | bytes 49160 | tf_op jit(solution)/shard_map/ppermute | solution.py:22
  339.0 38.1 %collective-permute-start.24 = (f32[64,64]{1,0:T(8,128)S(1)}, f32[64,64]{1,0:T(8,128)S(1)}, u32[]{:S(2)}, u32[]{:S(2)}) collective-permute-start(f32[64,64]{1,0:T(8,128)S(1)} %get-tuple-element.63), channel_id=1, source_target_pairs={{0,1},{1,2},{2,3},{3,4},{4,5},{5,6},{6,7},{7,8},{8,9},{9,10},{10,1... | collective-permute-start | bytes 49160 | tf_op jit(solution)/shard_map/ppermute | solution.py:22
  342.4 40.6 %collective-permute-start.25 = (f32[64,64]{1,0:T(8,128)S(1)}, f32[64,64]{1,0:T(8,128)S(1)}, u32[]{:S(2)}, u32[]{:S(2)}) collective-permute-start(f32[64,64]{1,0:T(8,128)S(1)} %get-tuple-element.62), channel_id=1, source_target_pairs={{0,511},{1,0},{2,1},{3,2},{4,3},{5,4},{6,5},{7,6},{8,7},{9,8},{10,... | collective-permute-start | bytes 49160 | tf_op jit(solution)/shard_map/ppermute | solution.py:22
  349.3 37.6 %collective-permute-start.26 = (f32[64,64]{1,0:T(8,128)S(1)}, f32[64,64]{1,0:T(8,128)S(1)}, u32[]{:S(2)}, u32[]{:S(2)}) collective-permute-start(f32[64,64]{1,0:T(8,128)S(1)} %get-tuple-element.61), channel_id=1, source_target_pairs={{0,16},{1,17},{2,18},{3,19},{4,20},{5,21},{6,22},{7,23},{8,24},{9,... | collective-permute-start | bytes 49160 | tf_op jit(solution)/shard_map/ppermute | solution.py:22
  375.2 28.5 %collective-permute-start.28 = (f32[64,64]{1,0:T(8,128)S(1)}, f32[64,64]{1,0:T(8,128)S(1)}, u32[]{:S(2)}, u32[]{:S(2)}) collective-permute-start(f32[64,64]{1,0:T(8,128)S(1)} %get-tuple-element.59), channel_id=1, source_target_pairs={{0,17},{1,18},{2,19},{3,20},{4,21},{5,22},{6,23},{7,24},{8,25},{9,... | collective-permute-start | bytes 49160 | tf_op jit(solution)/shard_map/ppermute | solution.py:22
  377.1 28.5 %collective-permute-start.29 = (f32[64,64]{1,0:T(8,128)S(1)}, f32[64,64]{1,0:T(8,128)S(1)}, u32[]{:S(2)}, u32[]{:S(2)}) collective-permute-start(f32[64,64]{1,0:T(8,128)S(1)} %get-tuple-element.58), channel_id=1, source_target_pairs={{0,15},{1,16},{2,17},{3,18},{4,19},{5,20},{6,21},{7,22},{8,23},{9,... | collective-permute-start | bytes 49160 | tf_op jit(solution)/shard_map/ppermute | solution.py:22
  394.2 34.0 %collective-permute-start.56 = (f32[64,64]{0,1:T(8,128)S(1)}, f32[64,64]{0,1:T(8,128)S(1)}, u32[]{:S(2)}, u32[]{:S(2)}) collective-permute-start(f32[64,64]{0,1:T(8,128)S(1)} %get-tuple-element.22), channel_id=1, source_target_pairs={{0,511},{1,0},{2,1},{3,2},{4,3},{5,4},{6,5},{7,6},{8,7},{9,8},{10,... | collective-permute-start | bytes 49160 | tf_op jit(solution)/shard_map/ppermute | solution.py:22
  405.7 34.0 %collective-permute-start.58 = (f32[64,64]{0,1:T(8,128)S(1)}, f32[64,64]{0,1:T(8,128)S(1)}, u32[]{:S(2)}, u32[]{:S(2)}) collective-permute-start(f32[64,64]{0,1:T(8,128)S(1)} %get-tuple-element.20), channel_id=1, source_target_pairs={{0,496},{1,497},{2,498},{3,499},{4,500},{5,501},{6,502},{7,503},{8... | collective-permute-start | bytes 49160 | tf_op jit(solution)/shard_map/ppermute | solution.py:22
  407.6 34.0 %collective-permute-start.59 = (f32[64,64]{0,1:T(8,128)S(1)}, f32[64,64]{0,1:T(8,128)S(1)}, u32[]{:S(2)}, u32[]{:S(2)}) collective-permute-start(f32[64,64]{0,1:T(8,128)S(1)} %get-tuple-element.19), channel_id=1, source_target_pairs={{0,16},{1,17},{2,18},{3,19},{4,20},{5,21},{6,22},{7,23},{8,24},{9,... | collective-permute-start | bytes 49160 | tf_op jit(solution)/shard_map/ppermute | solution.py:22
  411.0 30.6 %collective-permute-start.60 = (f32[64,64]{0,1:T(8,128)S(1)}, f32[64,64]{0,1:T(8,128)S(1)}, u32[]{:S(2)}, u32[]{:S(2)}) collective-permute-start(f32[64,64]{0,1:T(8,128)S(1)} %get-tuple-element.18), channel_id=1, source_target_pairs={{0,495},{1,496},{2,497},{3,498},{4,499},{5,500},{6,501},{7,502},{8... | collective-permute-start | bytes 49160 | tf_op jit(solution)/shard_map/ppermute | solution.py:22
  (88 other events, 8080.4 us)
Sparse Core Ops, SparseCore 0:
  452.3 256.5 all-reduce.5
where the time goes:
time: 728 us; the launch traced here: 718 us
  starting transfers between devices  294 us (40%)
  waiting for transfers between devices  265 us (36%)
  other arithmetic  91 us (12%)
  local copies, waits for them, and re-layouts  48 us (7%)
  between operations  17.7 us (2%)
    ppermute x64, starting transfers between devices, shifted(): lax.ppermute(value, axis, [(i, (i + by) % length) for i in range(length)])  294 us
    psum x1, waiting for transfers between devices, local(): weight_gradient = lax.psum(local_grad, 'pix') / math.sqrt(total_pixels)  256 us
    scatter-add x36, other arithmetic, adjoint_pieces(): spread.at[:, neighbours[stencil_slot]]  74 us
    gather x64, local copies, waits for them, and re-layouts, local(): extended[:, neighbours[forward_stencil_slot]]  28.2 us
  transfers between devices with their start and end apart: 65, of which 4 were waited for; matrix products, arithmetic and copies ran while one was open for 13% of the time, Pallas kernels for 0%

commit v1 on v0

v1 whole, which is shorter than its diff:
```python
import math

import jax
import jax.numpy as jnp
from jax import lax
from jax.experimental import pallas as pl
from jax.experimental.pallas import tpu as pltpu
from jax.sharding import PartitionSpec as P

CH = 64
KTERMS = 5
PIX = 256
HALO = 64
ROW = 16
PEERS = 8
STENCIL = 9
STEPS = KTERMS - 1
OFFSETS = [1, -1, 16, -16, 17, 15, -15, -17]
ORDER = [0, 1, 2, 3, 4, 7, 5, 6]
PART = 10
MESH = pl.DeviceIdType.MESH
F32 = jnp.float32
BF16 = jnp.bfloat16


def split(value):
    high = value.astype(BF16)
    return high, (value - high.astype(F32)).astype(BF16)


def dot(a, b):
    return jnp.dot(a, b, preferred_element_type=F32)


def dot_nt(a, b):
    return lax.dot_general(a, b, (((1,), (1,)), ((), ())), preferred_element_type=F32)


def product(value, high, low, times):
    value_high, value_low = split(value)
    both = times(jnp.concatenate([value_high, value_low], axis=0), high)
    result = both[:CH] + both[CH:]
    if low is not None:
        result = result + times(value_high, low)
    return result


def kernel(
    count,
    x_ref,
    w_ref,
    ct_ref,
    nb_ref,
    lw_ref,
    sends_ref,
    out_ref,
    mg_ref,
    wg_ref,
    a_high,
    a_low,
    h_high,
    h_low,
    s_mat,
    outgoing,
    incoming,
    sums,
    row_in,
    part,
    column_in,
    total,
    halo_send,
    halo_recv,
    row_send,
    row_recv,
    column_send,
    column_recv,
    last_send,
    last_recv,
):
    me = lax.axis_index("pix")
    rows = count // ROW
    my_row, my_column = me // ROW, me % ROW
    peers = [(me + OFFSETS[o] + count) % count for o in ORDER]

    def row_peer(step):
        return (my_column + step) % ROW

    def column_peer(step):
        return (my_row + step) % rows

    barrier = pltpu.get_barrier_semaphore()
    for peer in peers:
        pl.semaphore_signal(barrier, inc=1, device_id=(peer,), device_id_type=MESH)

    @pl.loop(1, ROW)
    def _(step):
        target = my_row * ROW + row_peer(step)
        pl.semaphore_signal(barrier, inc=1, device_id=(target,), device_id_type=MESH)

    @pl.loop(1, rows)
    def _(step):
        target = column_peer(step) * ROW + my_column
        pl.semaphore_signal(barrier, inc=1, device_id=(target,), device_id_type=MESH)

    lane_low = lax.broadcasted_iota(jnp.int32, (CH, 128), 1) < HALO

    for pair in range(PEERS // 2):
        listed = jnp.concatenate(
            [sends_ref[ORDER[2 * pair + i] : ORDER[2 * pair + i] + 1, :] for i in range(2)], axis=1
        )
        pixel = lax.broadcasted_iota(jnp.int32, (PIX, 128), 0)
        s_mat[:, 128 * pair : 128 * pair + 128] = jnp.where(pixel == listed, 1.0, 0.0).astype(BF16)
    for place, o in enumerate(ORDER):
        slot = lax.broadcasted_iota(jnp.int32, (HALO, PIX), 0) + (PIX + HALO * o)
        block = jnp.where(slot == nb_ref[o + 1 : o + 2, :], lw_ref[o + 1 : o + 2, :], 0.0)
        high, low = split(block)
        h_high[HALO * place : HALO * place + HALO, :] = high
        h_low[HALO * place : HALO * place + HALO, :] = low
    for base in range(0, PIX, 32):
        column = lax.broadcasted_iota(jnp.int32, (32, PIX), 0) + base
        block = jnp.zeros((32, PIX), F32)
        for slot in range(STENCIL):
            block = block + jnp.where(
                column == nb_ref[slot : slot + 1, :], lw_ref[slot : slot + 1, :], 0.0
            )
        high, low = split(block)
        a_high[base : base + 32, :] = high
        a_low[base : base + 32, :] = low

    weights = [w_ref[CH * k : CH * k + CH, :] for k in range(KTERMS)]

    def out_term(k, term):
        turned = lax.dot_general(
            weights[k],
            term.astype(BF16),
            (((0,), (0,)), ((), ())),
            preferred_element_type=F32,
        )
        return turned

    def mg_term(k, term):
        high, low = split(term)
        return dot(weights[k], high) + dot(weights[k], low)

    def halo_copy(step, place):
        return pltpu.make_async_remote_copy(
            src_ref=outgoing.at[step, place],
            dst_ref=incoming.at[step, place],
            send_sem=halo_send.at[step, place],
            recv_sem=halo_recv.at[step, place],
            device_id=(peers[place],),
            device_id_type=MESH,
        )

    def row_copy(step):
        other = row_peer(step)
        return pltpu.make_async_remote_copy(
            src_ref=sums.at[other],
            dst_ref=row_in.at[my_column],
            send_sem=row_send.at[other],
            recv_sem=row_recv.at[my_column],
            device_id=(my_row * ROW + other,),
            device_id_type=MESH,
        )

    def row_arrival(step):
        other = row_peer(step)
        return pltpu.make_async_remote_copy(
            src_ref=sums.at[other],
            dst_ref=row_in.at[other],
            send_sem=row_send.at[other],
            recv_sem=row_recv.at[other],
            device_id=(my_row * ROW + other,),
            device_id_type=MESH,
        )

    def column_copy(step, arrival):
        other = column_peer(step)
        place = other if arrival else my_row
        return pltpu.make_async_remote_copy(
            src_ref=part,
            dst_ref=column_in.at[place],
            send_sem=column_send.at[other],
            recv_sem=column_recv.at[place],
            device_id=(other * ROW + my_column,),
            device_id_type=MESH,
        )

    def last_copy(step, arrival):
        other = row_peer(step)
        place = other if arrival else my_column
        return pltpu.make_async_remote_copy(
            src_ref=total.at[my_column],
            dst_ref=total.at[place],
            send_sem=last_send.at[other],
            recv_sem=last_recv.at[place],
            device_id=(my_row * ROW + other,),
            device_id_type=MESH,
        )

    xs = [x_ref[...].astype(F32)]
    cs = [ct_ref[...].astype(F32)]
    out_sum = out_term(0, xs[0])
    mg_sum = mg_term(0, cs[0])
    pl.semaphore_wait(barrier, PEERS + ROW - 1 + rows - 1)

    for step in range(STEPS):
        x, c = xs[-1], cs[-1]
        gathered = product(x, s_mat[...], None, dot)
        returned = product(c, h_high[...], h_low[...], dot_nt)
        for pair in range(PEERS // 2):
            forward = gathered[:, 128 * pair : 128 * pair + 128]
            back = returned[:, 128 * pair : 128 * pair + 128]
            outgoing[step, 2 * pair] = jnp.where(lane_low, forward, back)
            halo_copy(step, 2 * pair).start()
            outgoing[step, 2 * pair + 1] = jnp.where(lane_low, back, forward)
            halo_copy(step, 2 * pair + 1).start()
        if step == 2:
            scale = 1.0 / math.sqrt(count * PIX)
            c0 = cs[0].astype(BF16)
            early = dot_nt(jnp.concatenate([t.astype(BF16) for t in xs], axis=0), c0)
            c_high, c_low = split(jnp.concatenate([cs[1], cs[2]], axis=0))
            x_high, x_low = split(xs[2])
            late = dot_nt(x_high, c_high) + dot_nt(x_low, c_high) + dot_nt(x_high, c_low)
            p0, p1, p2 = early[:CH], early[CH : 2 * CH], early[2 * CH :]
            first = jnp.concatenate([p1, p2], axis=1) * scale
            second = (2.0 * late - jnp.concatenate([p1, p0], axis=1)) * scale
            third = jnp.concatenate([p0[:32], p0[32:]], axis=1) * scale
            for i in range(ROW):
                sums[i, 0:4, :] = first[4 * i : 4 * i + 4]
                sums[i, 4:8, :] = second[4 * i : 4 * i + 4]
                sums[i, 8:10, :] = third[2 * i : 2 * i + 2]

            @pl.loop(1, ROW)
            def _(i):
                row_copy(i).start()

            row_in[my_column] = sums[my_column]
        if step == 3:

            @pl.loop(1, ROW)
            def _(i):
                row_arrival(i).wait_recv()

            piece = row_in[0]
            for i in range(1, ROW):
                piece = piece + row_in[i]
            part[...] = piece
            column_in[my_row] = piece

            @pl.loop(1, rows)
            def _(i):
                column_copy(i, False).start()

        x_near = product(x, a_high[...], a_low[...], dot)
        c_near = product(c, a_high[...], a_low[...], dot_nt)
        if step:
            out_sum = out_sum + out_term(step, x)
            mg_sum = mg_sum + mg_term(step, c)
        x_far, c_far = [], []
        for pair in range(PEERS // 2):
            halo_copy(step, 2 * pair).wait_recv()
            halo_copy(step, 2 * pair + 1).wait_recv()
            one, two = incoming[step, 2 * pair], incoming[step, 2 * pair + 1]
            x_far.append(jnp.where(lane_low, one, two))
            c_far.append(jnp.where(lane_low, two, one))
        x_sum = x_near + product(jnp.concatenate(x_far, axis=1), h_high[...], h_low[...], dot)
        c_sum = c_near + product(jnp.concatenate(c_far, axis=1), s_mat[...], None, dot_nt)
        if step:
            x_sum = 2.0 * x_sum - xs[-2]
            c_sum = 2.0 * c_sum - cs[-2]
        xs.append(x_sum)
        cs.append(c_sum)

    @pl.loop(1, rows)
    def _(i):
        column_copy(i, True).wait_recv()

    piece = column_in[0]
    for i in range(1, rows):
        piece = piece + column_in[i]
    total[my_column] = piece

    @pl.loop(1, ROW)
    def _(i):
        last_copy(i, False).start()

    out_ref[...] = (out_sum + out_term(STEPS, xs[-1])).astype(BF16)
    mg_ref[...] = (mg_sum + mg_term(STEPS, cs[-1])).astype(BF16)

    @pl.loop(1, ROW)
    def _(i):
        last_copy(i, True).wait_recv()

    def half(pieces, side):
        return jnp.concatenate(pieces, axis=0)[:, CH * side : CH * side + CH]

    first = [total[i, 0:4, :] for i in range(ROW)]
    second = [total[i, 4:8, :] for i in range(ROW)]
    third = [total[i, 8:10, :] for i in range(ROW)]
    wg_ref[0, 0:32] = half(third, 0)
    wg_ref[0, 32:64] = half(third, 1)
    wg_ref[1] = half(first, 0)
    wg_ref[2] = half(first, 1)
    wg_ref[3] = half(second, 0)
    wg_ref[4] = half(second, 1)

    for step in range(STEPS):
        for place in range(PEERS):
            halo_copy(step, place).wait_send()

    @pl.loop(1, ROW)
    def _(i):
        row_copy(i).wait_send()
        last_copy(i, False).wait_send()

    @pl.loop(1, rows)
    def _(i):
        column_copy(i, False).wait_send()


def solution(mesh):
    count = mesh.shape["pix"]
    rows = count // ROW
    dma = pltpu.SemaphoreType.DMA

    def local(input_maps, cheb_weights, cotangent, neighbours, lap_weights, send_rows):
        def body(*refs):
            kernel(count, *refs)

        return pl.pallas_call(
            body,
            out_shape=(
                jax.ShapeDtypeStruct((CH, PIX), BF16),
                jax.ShapeDtypeStruct((CH, PIX), BF16),
                jax.ShapeDtypeStruct((KTERMS, CH, CH), F32),
            ),
            in_specs=[pl.BlockSpec(memory_space=pltpu.VMEM)] * 6,
            out_specs=tuple([pl.BlockSpec(memory_space=pltpu.VMEM)] * 3),
            scratch_shapes=[
                pltpu.VMEM((PIX, PIX), BF16),
                pltpu.VMEM((PIX, PIX), BF16),
                pltpu.VMEM((PEERS * HALO, PIX), BF16),
                pltpu.VMEM((PEERS * HALO, PIX), BF16),
                pltpu.VMEM((PIX, PEERS * HALO), BF16),
                pltpu.VMEM((STEPS, PEERS, CH, 128), F32),
                pltpu.VMEM((STEPS, PEERS, CH, 128), F32),
                pltpu.VMEM((ROW, PART, 128), F32),
                pltpu.VMEM((ROW, PART, 128), F32),
                pltpu.VMEM((PART, 128), F32),
                pltpu.VMEM((rows, PART, 128), F32),
                pltpu.VMEM((ROW, PART, 128), F32),
                dma((STEPS, PEERS)),
                dma((STEPS, PEERS)),
                dma((ROW,)),
                dma((ROW,)),
                dma((rows,)),
                dma((rows,)),
                dma((ROW,)),
                dma((ROW,)),
            ],
            compiler_params=pltpu.CompilerParams(
                collective_id=0, has_side_effects=True, vmem_limit_bytes=32 * 1024 * 1024
            ),
        )(
            input_maps,
            cheb_weights.reshape(KTERMS * CH, CH),
            cotangent,
            neighbours,
            lap_weights,
            send_rows,
        )

    return jax.shard_map(
        local,
        mesh=mesh,
        in_specs=(
            P(None, "pix"),
            P(),
            P(None, "pix"),
            P(None, "pix"),
            P(None, "pix"),
            P("pix", None),
        ),
        out_specs=(P(None, "pix"), P(None, "pix"), P()),
        check_vma=False,
    )
```

time: 728 us -> 59 us (0.08); the launches traced: 718 us -> 58.6 us
  starting transfers between devices: 294 us -> 0 us
  waiting for transfers between devices: 265 us -> 0 us
  other arithmetic: 91 us -> 0 us
  Pallas kernels: 0 us -> 51.5 us
  local copies, waits for them, and re-layouts: 48 us -> 6.41 us
  between operations: 17.7 us -> 0.65 us
    ppermute x64 -> x0, starting transfers between devices: 294 us -> none  [shifted(): lax.ppermute(value, axis, [(i, (i + by) % length) for i in range(length)])]
    psum x1 -> x0, waiting for transfers between devices: 256 us -> none  [local(): weight_gradient = lax.psum(local_grad, 'pix') / math.sqrt(total_pixels)]
    scatter-add x40 -> x0, other arithmetic: 87.8 us -> none  [the longest x36 74 us: adjoint_pieces(): spread.at[:, neighbours[stencil_slot]]]
    pallas_call x0 -> x1, Pallas kernels: none -> 51.5 us  [local(): pl.pallas_call(body, out_shape=(jax.ShapeDtypeStruct((CH, PIX), BF16), ja...]
    gather x80 -> x0, local copies, waits for them, and re-layouts: 36.2 us -> none  [the longest x64 28.2 us: local(): extended[:, neighbours[forward_stencil_slot]]]
    ppermute x64 -> x0, waiting for transfers between devices: 8.62 us -> none  [shifted(): lax.ppermute(value, axis, [(i, (i + by) % length) for i in range(length)])]
  transfers between devices with their start and end apart: 65 -> 0, of which waited for: 4 -> 0; matrix products, arithmetic and copies ran while one was open for 13% -> 0% of each run, Pallas kernels for 0% -> 0%
where the time goes in v1:
time: 59 us; the launch traced here: 58.6 us
  Pallas kernels  51.5 us (87%)
  local copies, waits for them, and re-layouts  6.41 us (11%)
  between operations  0.65 us (1%)
    pallas_call x1, Pallas kernels, local(): pl.pallas_call(body, out_shape=(jax.ShapeDtypeStruct((CH, PIX), BF16), ja...  51.5 us
    unnamed x15, local copies, waits for them, and re-layouts  6.41 us

profile of v1, /device:TPU:1, one launch (start us, length us, event | category | flops | bytes accessed | tf_op | source)
XLA Modules:
  0.0 58.6 jit_solution(1285684733095722481)
XLA Ops:
  0.6 0.0 copy-start
  0.6 0.9 %copy-done = bf16[5,64,64]{2,1,0:T(8,128)(2,1)S(1)} copy-done((bf16[5,64,64]{2,1,0:T(8,128)(2,1)S(1)}, bf16[5,64,64]{2,1,0:T(8,128)(2,1)}, u32[]{:S(2)}) %copy-start) | copy-done | bytes 40984
  1.5 0.0 copy-start.1
  1.5 0.8 %copy-done.1 = bf16[64,256]{1,0:T(8,128)(2,1)S(1)} copy-done((bf16[64,256]{1,0:T(8,128)(2,1)S(1)}, bf16[64,256]{1,0:T(8,128)(2,1)}, u32[]{:S(2)}) %copy-start.1) | copy-done | bytes 32792
  2.3 0.0 copy-start.2
  2.3 0.8 %copy-done.2 = bf16[64,256]{1,0:T(8,128)(2,1)S(1)} copy-done((bf16[64,256]{1,0:T(8,128)(2,1)S(1)}, bf16[64,256]{1,0:T(8,128)(2,1)}, u32[]{:S(2)}) %copy-start.2) | copy-done | bytes 32792
  3.0 0.0 copy-start.3
  3.0 0.7 %copy-done.3 = s32[9,256]{1,0:T(8,128)S(1)} copy-done((s32[9,256]{1,0:T(8,128)S(1)}, s32[9,256]{1,0:T(8,128)}, u32[]{:S(2)}) %copy-start.3) | copy-done | bytes 9240
  3.8 0.0 copy-start.4
  3.8 0.7 %copy-done.4 = f32[9,256]{1,0:T(8,128)S(1)} copy-done((f32[9,256]{1,0:T(8,128)S(1)}, f32[9,256]{1,0:T(8,128)}, u32[]{:S(2)}) %copy-start.4) | copy-done | bytes 9240
  4.5 0.0 copy-start.5
  4.5 0.7 %copy-done.5 = s32[8,64]{1,0:T(8,128)S(1)} copy-done((s32[8,64]{1,0:T(8,128)S(1)}, s32[8,64]{1,0:T(8,128)}, u32[]{:S(2)}) %copy-start.5) | copy-done | bytes 2072
  5.2 51.5 %shard_map.85 = (bf16[64,256]{1,0:T(8,128)(2,1)S(1)}, bf16[64,256]{1,0:T(8,128)(2,1)S(1)}, f32[5,64,64]{2,1,0:T(8,128)S(1)}) custom-call(bf16[64,256]{1,0:T(8,128)(2,1)S(1)} %copy-done.1, bf16[320,64]{1,0:T(8,128)(2,1)S(1)} %bitcast.1, bf16[64,256]{1,0:T(8,128)(2,1)S(1)} %copy-done.2, s32[9,256]{1,0:T(8,128)S(1)} %copy-done.3, f32[9,256]{1,0:T(8,128)S(1)} %copy-done.4, ...), custom_call_target="tpu_custom_call" | custom-call | tf_op jit(solution)/shard_map/pallas_call | solution.py:331
  56.7 0.6 %copy.12 = bf16[64,256]{1,0:T(8,128)(2,1)} copy(bf16[64,256]{1,0:T(8,128)(2,1)S(1)} %get-tuple-element.6) | data formatting | bytes 65536
  57.3 0.6 %copy.13 = bf16[64,256]{1,0:T(8,128)(2,1)} copy(bf16[64,256]{1,0:T(8,128)(2,1)S(1)} %get-tuple-element.7) | data formatting | bytes 65536
  57.9 0.7 %copy.14 = f32[5,64,64]{2,1,0:T(8,128)} copy(f32[5,64,64]{2,1,0:T(8,128)S(1)} %get-tuple-element.8) | data formatting | bytes 163840
Async XLA Ops:
  0.6 0.9 %copy-start = (bf16[5,64,64]{2,1,0:T(8,128)(2,1)S(1)}, bf16[5,64,64]{2,1,0:T(8,128)(2,1)}, u32[]{:S(2)}) copy-start(bf16[5,64,64]{2,1,0:T(8,128)(2,1)} %param.7) | copy-start | bytes 122884
  1.5 0.8 %copy-start.1 = (bf16[64,256]{1,0:T(8,128)(2,1)S(1)}, bf16[64,256]{1,0:T(8,128)(2,1)}, u32[]{:S(2)}) copy-start(bf16[64,256]{1,0:T(8,128)(2,1)} %refs_0_.1) | copy-start | bytes 98308
  2.3 0.8 %copy-start.2 = (bf16[64,256]{1,0:T(8,128)(2,1)S(1)}, bf16[64,256]{1,0:T(8,128)(2,1)}, u32[]{:S(2)}) copy-start(bf16[64,256]{1,0:T(8,128)(2,1)} %refs_2_.1) | copy-start | bytes 98308
  3.0 0.7 %copy-start.3 = (s32[9,256]{1,0:T(8,128)S(1)}, s32[9,256]{1,0:T(8,128)}, u32[]{:S(2)}) copy-start(s32[9,256]{1,0:T(8,128)} %refs_3_.1) | copy-start | bytes 27652
  3.8 0.7 %copy-start.4 = (f32[9,256]{1,0:T(8,128)S(1)}, f32[9,256]{1,0:T(8,128)}, u32[]{:S(2)}) copy-start(f32[9,256]{1,0:T(8,128)} %refs_4_.1) | copy-start | bytes 27652
  4.5 0.7 %copy-start.5 = (s32[8,64]{1,0:T(8,128)S(1)}, s32[8,64]{1,0:T(8,128)}, u32[]{:S(2)}) copy-start(s32[8,64]{1,0:T(8,128)} %refs_5_.1) | copy-start | bytes 6148

commit v2 on v0

v2 whole, which is shorter than its diff:
```python
import math

import jax
import jax.numpy as jnp
from jax import lax
from jax.experimental import pallas as pl
from jax.experimental.pallas import tpu as pltpu
from jax.sharding import PartitionSpec as P

CH = 64
KTERMS = 5
PIX = 256
HALO = 64
ROW = 16
PEERS = 8
STENCIL = 9
STEPS = KTERMS - 1
OFFSETS = [1, -1, 16, -16, 17, 15, -15, -17]
ORDER = [0, 1, 2, 3, 4, 7, 5, 6]
LISTED = PEERS * HALO
SHARES = [6, 4]
MESH = pl.DeviceIdType.MESH
F32 = jnp.float32
BF16 = jnp.bfloat16


def split(value):
    high = value.astype(BF16)
    return high, (value - high.astype(F32)).astype(BF16)


def dot(a, b):
    return jnp.dot(a, b, preferred_element_type=F32)


def dot_nt(a, b):
    return lax.dot_general(a, b, (((1,), (1,)), ((), ())), preferred_element_type=F32)


def dot_tn(a, b):
    return lax.dot_general(a, b, (((0,), (0,)), ((), ())), preferred_element_type=F32)


def product(value, matrix, times):
    high, low = split(value)
    both = times(jnp.concatenate([high, low], axis=0), matrix)
    rows = value.shape[0]
    return both[:rows] + both[rows:]


def turned(value):
    return pltpu.roll(value, HALO, 1)


def kernel(
    count,
    x_hbm,
    w_hbm,
    ct_hbm,
    nb_hbm,
    lw_hbm,
    sends_hbm,
    out_ref,
    mg_ref,
    wg_ref,
    x_ref,
    w_ref,
    ct_ref,
    nb_ref,
    lw_ref,
    sends_ref,
    load_sem,
    a_high,
    a_low,
    s_mat,
    t_mat,
    outgoing,
    incoming,
    halo_send,
    halo_recv,
    sum_send,
    sum_recv,
    *sum_refs,
):
    me = lax.axis_index("pix")
    rows = count // ROW
    my_row, my_column = me // ROW, me % ROW
    peers = [(me + OFFSETS[o] + count) % count for o in ORDER]

    def in_row(step):
        return my_row * ROW + (my_column + step) % ROW

    def in_column(step):
        return (my_row + step) % rows * ROW + my_column

    barrier = pltpu.get_barrier_semaphore()

    def greet(device):
        pl.semaphore_signal(barrier, inc=1, device_id=(device,), device_id_type=MESH)

    for peer in peers:
        greet(peer)
    greet(in_row(1))
    greet(in_row(ROW - 1))

    loads = [
        pltpu.make_async_copy(src, dst, load_sem.at[i])
        for i, (src, dst) in enumerate(
            (
                (sends_hbm, sends_ref),
                (x_hbm, x_ref),
                (nb_hbm, nb_ref),
                (lw_hbm, lw_ref),
                (ct_hbm, ct_ref),
                (w_hbm, w_ref),
            )
        )
    ]
    for load in loads:
        load.start()

    @pl.loop(2, rows - 1)
    def _(step):
        greet(in_column(step))

    @pl.loop(2, ROW - 1)
    def _(step):
        greet(in_row(step))

    lane_low = lax.broadcasted_iota(jnp.int32, (CH // 2, 128), 1) < HALO

    def halo_copy(chain, step, place):
        return pltpu.make_async_remote_copy(
            src_ref=outgoing.at[chain, step, place],
            dst_ref=incoming.at[chain, step, place],
            send_sem=halo_send.at[chain, step],
            recv_sem=halo_recv.at[chain, step],
            device_id=(peers[place if chain == 0 else place ^ 1],),
            device_id_type=MESH,
        )

    def halo_all(chain, step):
        return pltpu.make_async_remote_copy(
            src_ref=outgoing.at[chain, step],
            dst_ref=incoming.at[chain, step],
            send_sem=halo_send.at[chain, step],
            recv_sem=halo_recv.at[chain, step],
            device_id=(peers[0],),
            device_id_type=MESH,
        )

    def post(chain, step, columns, start=True):
        for pair in range(PEERS // 2):
            block = columns[:, 128 * pair : 128 * pair + 128]
            upper, lower = block[: CH // 2], block[CH // 2 :]
            outgoing[chain, step, 2 * pair] = jnp.where(lane_low, upper, turned(lower))
            outgoing[chain, step, 2 * pair + 1] = jnp.where(lane_low, turned(upper), lower)
            if start:
                halo_copy(chain, step, 2 * pair).start()
                halo_copy(chain, step, 2 * pair + 1).start()

    def collect(chain, step):
        halo_all(chain, step).wait_recv()
        blocks = []
        for pair in range(PEERS // 2):
            one, two = incoming[chain, step, 2 * pair], incoming[chain, step, 2 * pair + 1]
            blocks.append(
                jnp.concatenate(
                    [jnp.where(lane_low, one, turned(two)), jnp.where(lane_low, turned(one), two)],
                    axis=0,
                )
            )
        return jnp.concatenate(blocks, axis=1)

    loads[0].wait()
    pixel = lax.broadcasted_iota(jnp.int32, (PIX, 128), 0)
    for pair in range(PEERS // 2):
        listed = jnp.concatenate(
            [sends_ref[ORDER[2 * pair + i] : ORDER[2 * pair + i] + 1, :] for i in range(2)], axis=1
        )
        s_mat[:, 128 * pair : 128 * pair + 128] = jnp.where(pixel == listed, 1.0, 0.0).astype(BF16)
    loads[1].wait()
    xs = [x_ref[...].astype(F32)]
    post(0, 0, dot(x_ref[...], s_mat[...]), start=False)
    loads[2].wait()
    slot = lax.broadcasted_iota(jnp.int32, (HALO, PIX), 0) + PIX
    for place, o in enumerate(ORDER):
        hit = slot + HALO * o == nb_ref[o + 1 : o + 2, :]
        t_mat[HALO * place : HALO * place + HALO, :] = jnp.where(hit, 1.0, 0.0).astype(BF16)
    loads[3].wait()
    lists = jnp.concatenate([lw_ref[o + 1 : o + 2, :] for o in ORDER], axis=0)
    high, rest = split(lists)
    middle = (lists - high.astype(F32)).astype(BF16)
    low = (lists - high.astype(F32) - middle.astype(F32)).astype(BF16)
    found = dot_nt(jnp.concatenate([high, middle, low], axis=0), t_mat[...])
    found = found[:PEERS] + found[PEERS : 2 * PEERS] + found[2 * PEERS :]
    own = lax.broadcasted_iota(jnp.int32, (PEERS, LISTED), 1) // HALO
    own = own == lax.broadcasted_iota(jnp.int32, (PEERS, LISTED), 0)
    list_weight = jnp.sum(jnp.where(own, found, 0.0), axis=0, keepdims=True)
    loads[4].wait()
    cs = [ct_ref[...].astype(F32)]
    post(1, 0, dot_nt(ct_ref[...], t_mat[...]) * list_weight, start=False)
    pl.semaphore_wait(barrier, PEERS + ROW - 1 + rows - 3)
    for chain in range(2):
        for place in range(PEERS):
            halo_copy(chain, 0, place).start()

    for base in range(0, PIX, 32):
        column = lax.broadcasted_iota(jnp.int32, (32, PIX), 0) + base
        block = jnp.zeros((32, PIX), F32)
        for entry in range(STENCIL):
            block = block + jnp.where(
                column == nb_ref[entry : entry + 1, :], lw_ref[entry : entry + 1, :], 0.0
            )
        high, low = split(block)
        a_high[base : base + 32, :] = high
        a_low[base : base + 32, :] = low
    loads[5].wait()

    def near(value, times):
        return product(value, a_high[...], times) + times(value.astype(BF16), a_low[...])

    def out_term(k):
        return dot_tn(w_ref[CH * k : CH * k + CH, :], xs[k].astype(BF16))

    def mg_term(k):
        high, low = split(cs[k])
        weight = w_ref[CH * k : CH * k + CH, :]
        return dot(weight, high) + dot(weight, low)

    def inner(x, c):
        x_high, x_low = split(x)
        c_high, c_low = split(c)
        both = dot_nt(jnp.concatenate([x_high, x_low], axis=0), c_high)
        return both[:CH] + both[CH:] + dot_nt(x_high, c_low)

    class Batch:
        def __init__(self, which):
            self.which = which
            self.sums, self.row_in, self.part, self.column_in, self.total = sum_refs[
                5 * which : 5 * which + 5
            ]

        def copy(self, stage, src, dst, device):
            return pltpu.make_async_remote_copy(
                src_ref=src,
                dst_ref=dst,
                send_sem=sum_send.at[self.which, stage],
                recv_sem=sum_recv.at[self.which, stage],
                device_id=(device,),
                device_id_type=MESH,
            )

        def all_of(self, stage):
            ref = (self.row_in, self.column_in, self.total)[stage]
            ref = ref.at[pl.ds(0, (ROW, rows, ROW)[stage] - 1)]
            return self.copy(stage, ref, ref, peers[0])

        def start(self, blocks):
            at = 0
            for block in blocks:
                n = block.shape[0] // ROW
                for i in range(ROW):
                    self.sums[i, at : at + n, :] = block[n * i : n * i + n]
                at += n

            @pl.loop(1, ROW)
            def _(i):
                other = (my_column + i) % ROW
                self.copy(
                    0, self.sums.at[other], self.row_in.at[my_column], my_row * ROW + other
                ).start()

            self.row_in[my_column] = self.sums[my_column]

        def across(self):
            self.all_of(0).wait_recv()
            piece = self.row_in[0]
            for i in range(1, ROW):
                piece = piece + self.row_in[i]
            self.part[...] = piece

            @pl.loop(1, rows)
            def _(i):
                self.copy(1, self.part, self.column_in.at[my_row], in_column(i)).start()

            self.column_in[my_row] = piece

        def back(self):
            self.all_of(1).wait_recv()
            piece = self.column_in[0]
            for i in range(1, rows):
                piece = piece + self.column_in[i]
            self.total[my_column] = piece

            @pl.loop(1, ROW)
            def _(i):
                mine = self.total.at[my_column]
                self.copy(2, mine, mine, in_row(i)).start()

        def arrive(self):
            self.all_of(2).wait_recv()

        def end(self):
            for stage in range(3):
                self.all_of(stage).wait_send()

    early, late = Batch(0), Batch(1)
    scale = 1.0 / math.sqrt(count * PIX)

    def halves(value):
        return jnp.concatenate([value[: CH // 2], value[CH // 2 :]], axis=1)

    out_sum = mg_sum = None
    for step in range(STEPS):
        x_near = near(xs[step], dot)
        c_near = near(cs[step], dot_nt)
        x_next = x_near + product(collect(0, step) * list_weight, t_mat[...], dot)
        if step:
            x_next = 2.0 * x_next - xs[step - 1]
        xs.append(x_next)
        if step + 1 < STEPS:
            post(0, step + 1, product(x_next, s_mat[...], dot))
        c_next = c_near + product(collect(1, step), s_mat[...], dot_nt)
        if step:
            c_next = 2.0 * c_next - cs[step - 1]
        cs.append(c_next)
        if step + 1 < STEPS:
            post(1, step + 1, product(c_next, t_mat[...], dot_nt) * list_weight)
        if step == 0:
            p0 = dot_nt(x_ref[...], ct_ref[...]) * scale
            p1 = dot_nt(xs[1].astype(BF16), ct_ref[...]) * scale
            p2 = inner(xs[1], cs[1]) * (2.0 * scale) - p0
            early.start([jnp.concatenate([p0, p1], axis=1), halves(p2)])
        if step == 1:
            last = inner(xs[2], jnp.concatenate([cs[1], cs[2]], axis=0)) * (2.0 * scale)
            late.start([last - jnp.concatenate([p1, p0], axis=1)])
            early.across()
        if step == 2:
            late.across()
            early.back()
        term_out, term_mg = out_term(step), mg_term(step)
        out_sum = term_out if out_sum is None else out_sum + term_out
        mg_sum = term_mg if mg_sum is None else mg_sum + term_mg

    out_ref[...] = (out_sum + out_term(STEPS)).astype(BF16)
    mg_ref[...] = (mg_sum + mg_term(STEPS)).astype(BF16)
    late.back()
    early.arrive()

    def rows_of(batch, lower, upper):
        return jnp.concatenate([batch.total[i, lower:upper, :] for i in range(ROW)], axis=0)

    first = rows_of(early, 0, 4)
    third = rows_of(early, 4, 6)
    wg_ref[0] = first[:, :CH]
    wg_ref[1] = first[:, CH:]
    wg_ref[2, : CH // 2] = third[:, :CH]
    wg_ref[2, CH // 2 :] = third[:, CH:]
    for chain in range(2):
        for step in range(STEPS):
            halo_all(chain, step).wait_send()
    early.end()
    late.arrive()
    second = rows_of(late, 0, 4)
    wg_ref[3] = second[:, :CH]
    wg_ref[4] = second[:, CH:]
    late.end()


def store_results(out_ref, mg_ref, wg_ref, out_hbm, mg_hbm, wg_hbm, sem):
    copies = [
        pltpu.make_async_copy(src, dst, sem.at[i])
        for i, (src, dst) in enumerate(((wg_ref, wg_hbm), (out_ref, out_hbm), (mg_ref, mg_hbm)))
    ]
    for copy in copies:
        copy.start()
    for copy in copies:
        copy.wait()


def solution(mesh):
    count = mesh.shape["pix"]
    rows = count // ROW
    dma = pltpu.SemaphoreType.DMA

    def local(input_maps, cheb_weights, cotangent, neighbours, lap_weights, send_rows):
        def body(*refs):
            kernel(count, *refs)

        results = pl.pallas_call(
            body,
            out_shape=(
                jax.ShapeDtypeStruct((CH, PIX), BF16),
                jax.ShapeDtypeStruct((CH, PIX), BF16),
                jax.ShapeDtypeStruct((KTERMS, CH, CH), F32),
            ),
            in_specs=[pl.BlockSpec(memory_space=pltpu.HBM)] * 6,
            out_specs=tuple([pl.BlockSpec(memory_space=pltpu.VMEM)] * 3),
            scratch_shapes=[
                pltpu.VMEM((CH, PIX), BF16),
                pltpu.VMEM((KTERMS * CH, CH), BF16),
                pltpu.VMEM((CH, PIX), BF16),
                pltpu.VMEM((STENCIL, PIX), jnp.int32),
                pltpu.VMEM((STENCIL, PIX), F32),
                pltpu.VMEM((PEERS, HALO), jnp.int32),
                dma((6,)),
                pltpu.VMEM((PIX, PIX), BF16),
                pltpu.VMEM((PIX, PIX), BF16),
                pltpu.VMEM((PIX, LISTED), BF16),
                pltpu.VMEM((LISTED, PIX), BF16),
                pltpu.VMEM((2, STEPS, PEERS, CH // 2, 128), F32),
                pltpu.VMEM((2, STEPS, PEERS, CH // 2, 128), F32),
                dma((2, STEPS)),
                dma((2, STEPS)),
                dma((2, 3)),
                dma((2, 3)),
                *[
                    pltpu.VMEM(lead + (share, 128), F32)
                    for share in SHARES
                    for lead in ((ROW,), (ROW,), (), (rows,), (ROW,))
                ],
            ],
            compiler_params=pltpu.CompilerParams(
                collective_id=0, has_side_effects=True, vmem_limit_bytes=60 * 1024 * 1024
            ),
        )(
            input_maps,
            cheb_weights.reshape(KTERMS * CH, CH),
            cotangent,
            neighbours,
            lap_weights,
            send_rows,
        )
        return pl.pallas_call(
            store_results,
            out_shape=tuple(jax.ShapeDtypeStruct(r.shape, r.dtype) for r in results),
            in_specs=[pl.BlockSpec(memory_space=pltpu.VMEM)] * 3,
            out_specs=tuple([pl.BlockSpec(memory_space=pltpu.HBM)] * 3),
            scratch_shapes=[dma((3,))],
        )(*results)

    return jax.shard_map(
        local,
        mesh=mesh,
        in_specs=(
            P(None, "pix"),
            P(),
            P(None, "pix"),
            P(None, "pix"),
            P(None, "pix"),
            P("pix", None),
        ),
        out_specs=(P(None, "pix"), P(None, "pix"), P()),
        check_vma=False,
    )
```

time: 728 us -> 49.5 us (0.07); the launches traced: 718 us -> 49.4 us
  starting transfers between devices: 294 us -> 0 us
  waiting for transfers between devices: 265 us -> 0 us
  other arithmetic: 91 us -> 0 us
  Pallas kernels: 0 us -> 48.7 us
  local copies, waits for them, and re-layouts: 48 us -> 0 us
  between operations: 17.7 us -> 0.64 us
    ppermute x64 -> x0, starting transfers between devices: 294 us -> none  [shifted(): lax.ppermute(value, axis, [(i, (i + by) % length) for i in range(length)])]
    psum x1 -> x0, waiting for transfers between devices: 256 us -> none  [local(): weight_gradient = lax.psum(local_grad, 'pix') / math.sqrt(total_pixels)]
    scatter-add x40 -> x0, other arithmetic: 87.8 us -> none  [the longest x36 74 us: adjoint_pieces(): spread.at[:, neighbours[stencil_slot]]]
    pallas_call x0 -> x2, Pallas kernels: none -> 48.7 us  [the longest x1 47.1 us: local(): pl.pallas_call(body, out_shape=(jax.ShapeDtypeStruct((CH, PIX), BF16), ja...]
    gather x80 -> x0, local copies, waits for them, and re-layouts: 36.2 us -> none  [the longest x64 28.2 us: local(): extended[:, neighbours[forward_stencil_slot]]]
    ppermute x64 -> x0, waiting for transfers between devices: 8.62 us -> none  [shifted(): lax.ppermute(value, axis, [(i, (i + by) % length) for i in range(length)])]
  transfers between devices with their start and end apart: 65 -> 0, of which waited for: 4 -> 0; matrix products, arithmetic and copies ran while one was open for 13% -> 0% of each run, Pallas kernels for 0% -> 0%
where the time goes in v2:
time: 49.5 us; the launch traced here: 49.4 us
  Pallas kernels  48.7 us (98%)
  between operations  0.64 us (1%)
    pallas_call x1, Pallas kernels, local(): pl.pallas_call(body, out_shape=(jax.ShapeDtypeStruct((CH, PIX), BF16), ja...  47.1 us
    pallas_call x1, Pallas kernels, local(): pl.pallas_call(store_results, out_shape=tuple((jax.ShapeDtypeStruct(r.sha...  1.66 us

profile of v2, /device:TPU:1, one launch (start us, length us, event | category | flops | bytes accessed | tf_op | source)
XLA Modules:
  0.0 49.4 jit_solution(4573784519792866020)
XLA Ops:
  0.6 47.1 %shard_map.85 = (bf16[64,256]{1,0:T(8,128)(2,1)}, bf16[64,256]{1,0:T(8,128)(2,1)}, f32[5,64,64]{2,1,0:T(8,128)}) custom-call(bf16[64,256]{1,0:T(8,128)(2,1)} %refs_0_.1, bf16[320,64]{1,0:T(8,128)(2,1)} %bitcast.1, bf16[64,256]{1,0:T(8,128)(2,1)} %refs_2_.1, s32[9,256]{1,0:T(8,128)} %refs_3_.1, f32[9,256]{1,0:T(8,128)} %refs_4_.1, s32[8,64]{1,0:T(8,128)} %refs_5_.1), custom_call_target="tpu_custom_call" | custom-call | tf_op jit(solution)/shard_map/pallas_call | solution.py:391
  47.7 1.7 %shard_map.86 = (bf16[64,256]{1,0:T(8,128)(2,1)}, bf16[64,256]{1,0:T(8,128)(2,1)}, f32[5,64,64]{2,1,0:T(8,128)}) custom-call(bf16[64,256]{1,0:T(8,128)(2,1)} %get-tuple-element.6.out_ref, bf16[64,256]{1,0:T(8,128)(2,1)} %get-tuple-element.7.mg_ref, f32[5,64,64]{2,1,0:T(8,128)} %get-tuple-element.8.wg_ref), custom_call_target="tpu_custom_call" | custom-call | tf_op jit(solution)/shard_map/pallas_call | solution.py:435

commit v3 on v2

--- a/solution.py
+++ b/solution.py
@@ -315,16 +315,25 @@
     for step in range(STEPS):
         x_near = near(xs[step], dot)
         c_near = near(cs[step], dot_nt)
+        if step == 2:
+            late.across()
+        if step == 3:
+            late.back()
+            early.back()
         x_next = x_near + product(collect(0, step) * list_weight, t_mat[...], dot)
         if step:
             x_next = 2.0 * x_next - xs[step - 1]
         xs.append(x_next)
-        if step + 1 < STEPS:
+        if step in (0, 2):
             post(0, step + 1, product(x_next, s_mat[...], dot))
         c_next = c_near + product(collect(1, step), s_mat[...], dot_nt)
         if step:
             c_next = 2.0 * c_next - cs[step - 1]
         cs.append(c_next)
+        if step == 1:
+            last = inner(xs[2], jnp.concatenate([cs[1], cs[2]], axis=0)) * (2.0 * scale)
+            late.start([last - jnp.concatenate([p1, p0], axis=1)])
+            post(0, step + 1, product(x_next, s_mat[...], dot))
         if step + 1 < STEPS:
             post(1, step + 1, product(c_next, t_mat[...], dot_nt) * list_weight)
         if step == 0:
@@ -333,19 +342,17 @@
             p2 = inner(xs[1], cs[1]) * (2.0 * scale) - p0
             early.start([jnp.concatenate([p0, p1], axis=1), halves(p2)])
         if step == 1:
-            last = inner(xs[2], jnp.concatenate([cs[1], cs[2]], axis=0)) * (2.0 * scale)
-            late.start([last - jnp.concatenate([p1, p0], axis=1)])
             early.across()
-        if step == 2:
-            late.across()
-            early.back()
-        term_out, term_mg = out_term(step), mg_term(step)
-        out_sum = term_out if out_sum is None else out_sum + term_out
-        mg_sum = term_mg if mg_sum is None else mg_sum + term_mg
-
-    out_ref[...] = (out_sum + out_term(STEPS)).astype(BF16)
-    mg_ref[...] = (mg_sum + mg_term(STEPS)).astype(BF16)
-    late.back()
+        if step < STEPS - 1:
+            term_out, term_mg = out_term(step), mg_term(step)
+            out_sum = term_out if out_sum is None else out_sum + term_out
+            mg_sum = term_mg if mg_sum is None else mg_sum + term_mg
+
+    for k in (STEPS - 1, STEPS):
+        out_sum = out_sum + out_term(k)
+        mg_sum = mg_sum + mg_term(k)
+    out_ref[...] = out_sum.astype(BF16)
+    mg_ref[...] = mg_sum.astype(BF16)
     early.arrive()
 
     def rows_of(batch, lower, upper):
@@ -391,9 +398,9 @@
         results = pl.pallas_call(
             body,
             out_shape=(
-                jax.ShapeDtypeStruct((CH, PIX), BF16),
-                jax.ShapeDtypeStruct((CH, PIX), BF16),
-                jax.ShapeDtypeStruct((KTERMS, CH, CH), F32),
+                pltpu.VMEM((CH, PIX), BF16),
+                pltpu.VMEM((CH, PIX), BF16),
+                pltpu.VMEM((KTERMS, CH, CH), F32),
             ),
             in_specs=[pl.BlockSpec(memory_space=pltpu.HBM)] * 6,
             out_specs=tuple([pl.BlockSpec(memory_space=pltpu.VMEM)] * 3),
@@ -422,15 +429,20 @@
                 ],
             ],
             compiler_params=pltpu.CompilerParams(
-                collective_id=0, has_side_effects=True, vmem_limit_bytes=60 * 1024 * 1024
+                collective_id=0, has_side_effects=True, vmem_limit_bytes=16 * 1024 * 1024
             ),
         )(
-            input_maps,
-            cheb_weights.reshape(KTERMS * CH, CH),
-            cotangent,
-            neighbours,
-            lap_weights,
-            send_rows,
+            *[
+                pltpu.with_memory_space_constraint(operand, pltpu.HBM)
+                for operand in (
+                    input_maps,
+                    cheb_weights.reshape(KTERMS * CH, CH),
+                    cotangent,
+                    neighbours,
+                    lap_weights,
+                    send_rows,
+                )
+            ]
         )
         return pl.pallas_call(
             store_results,
@@ -438,7 +450,7 @@
             in_specs=[pl.BlockSpec(memory_space=pltpu.VMEM)] * 3,
             out_specs=tuple([pl.BlockSpec(memory_space=pltpu.HBM)] * 3),
             scratch_shapes=[dma((3,))],
-        )(*results)
+        )(*[pltpu.with_memory_space_constraint(r, pltpu.VMEM) for r in results])
 
     return jax.shard_map(
         local,

time: 49.5 us -> 45.6 us (0.921)
  Pallas kernels: 48.7 us -> 44.8 us
    pallas_call x1, Pallas kernels: 47.1 us -> 44.1 us  [local(): pl.pallas_call(body, out_shape=(pltpu.VMEM((CH, PIX), BF16), pltpu.VMEM((...]
    pallas_call x1, Pallas kernels: 1.66 us -> 0.71 us  [local(): pl.pallas_call(store_results, out_shape=tuple((jax.ShapeDtypeStruct(r.sha...]
where the time goes in v3:
time: 45.6 us; the launch traced here: 45.4 us
  Pallas kernels  44.8 us (98%)
  between operations  0.64 us (1%)
    pallas_call x1, Pallas kernels, local(): pl.pallas_call(body, out_shape=(pltpu.VMEM((CH, PIX), BF16), pltpu.VMEM((...  44.1 us

profile of v3, /device:TPU:1, one launch (start us, length us, event | category | flops | bytes accessed | tf_op | source)
XLA Modules:
  0.0 45.4 jit_solution(8662932919707143029)
XLA Ops:
  0.6 44.1 %shard_map.85 = (bf16[64,256]{1,0:T(8,128)(2,1)S(1)}, bf16[64,256]{1,0:T(8,128)(2,1)S(1)}, f32[5,64,64]{2,1,0:T(8,128)S(1)}) custom-call(bf16[64,256]{1,0:T(8,128)(2,1)} %refs_0_.1, bf16[320,64]{1,0:T(8,128)(2,1)} %bitcast.1, bf16[64,256]{1,0:T(8,128)(2,1)} %refs_2_.1, s32[9,256]{1,0:T(8,128)} %refs_3_.1, f32[9,256]{1,0:T(8,128)} %refs_4_.1, s32[8,64]{1,0:T(8,128)} %refs_5_.1), custom_call_target="tpu_custom_call" | custom-call | tf_op jit(solution)/shard_map/pallas_call | solution.py:398
  44.7 0.7 %shard_map.86 = (bf16[64,256]{1,0:T(8,128)(2,1)}, bf16[64,256]{1,0:T(8,128)(2,1)}, f32[5,64,64]{2,1,0:T(8,128)}) custom-call(bf16[64,256]{1,0:T(8,128)(2,1)S(1)} %get-tuple-element.6.out_ref, bf16[64,256]{1,0:T(8,128)(2,1)S(1)} %get-tuple-element.7.mg_ref, f32[5,64,64]{2,1,0:T(8,128)S(1)} %get-tuple-element.8.wg_ref), custom_call_target="tpu_custom_call" | custom-call | tf_op jit(solution)/shard_map/pallas_call | solution.py:447

commit v4 on v3

--- a/solution.py
+++ b/solution.py
@@ -70,6 +70,7 @@
     lw_ref,
     sends_ref,
     load_sem,
+    known,
     a_high,
     a_low,
     s_mat,
@@ -100,8 +101,8 @@
 
     for peer in peers:
         greet(peer)
-    greet(in_row(1))
-    greet(in_row(ROW - 1))
+    for step in (1, ROW - 1):
+        greet(in_row(step))
 
     loads = [
         pltpu.make_async_copy(src, dst, load_sem.at[i])
@@ -119,13 +120,16 @@
     for load in loads:
         load.start()
 
-    @pl.loop(2, rows - 1)
-    def _(step):
-        greet(in_column(step))
-
-    @pl.loop(2, ROW - 1)
-    def _(step):
-        greet(in_row(step))
+    def spread(k):
+        for ring, size in ((in_row, ROW), (in_column, rows)):
+            if 4 * 2**k <= size:
+                for other in (2**k, size - 2**k):
+                    pl.semaphore_signal(
+                        known.at[k], inc=1, device_id=(ring(other),), device_id_type=MESH
+                    )
+
+    def heard(k):
+        pl.semaphore_wait(known.at[k], sum(2 for size in (ROW, rows) if 4 * 2**k <= size))
 
     lane_low = lax.broadcasted_iota(jnp.int32, (CH // 2, 128), 1) < HALO
 
@@ -200,10 +204,11 @@
     loads[4].wait()
     cs = [ct_ref[...].astype(F32)]
     post(1, 0, dot_nt(ct_ref[...], t_mat[...]) * list_weight, start=False)
-    pl.semaphore_wait(barrier, PEERS + ROW - 1 + rows - 3)
+    pl.semaphore_wait(barrier, PEERS + 2)
     for chain in range(2):
         for place in range(PEERS):
             halo_copy(chain, 0, place).start()
+    spread(0)
 
     for base in range(0, PIX, 32):
         column = lax.broadcasted_iota(jnp.int32, (32, PIX), 0) + base
@@ -320,28 +325,42 @@
         if step == 3:
             late.back()
             early.back()
+        if step == 0:
+            heard(0)
+            spread(1)
+            heard(1)
+            spread(2)
         x_next = x_near + product(collect(0, step) * list_weight, t_mat[...], dot)
         if step:
             x_next = 2.0 * x_next - xs[step - 1]
         xs.append(x_next)
+        if step + 1 < STEPS:
+            listed = product(x_next, s_mat[...], dot)
         if step in (0, 2):
-            post(0, step + 1, product(x_next, s_mat[...], dot))
+            post(0, step + 1, listed)
+        if step == 1:
+            none = jnp.zeros((CH, PIX), F32)
+            last = inner(x_next, jnp.concatenate([cs[1], none], axis=0)) - half_early
         c_next = c_near + product(collect(1, step), s_mat[...], dot_nt)
         if step:
             c_next = 2.0 * c_next - cs[step - 1]
         cs.append(c_next)
         if step == 1:
-            last = inner(xs[2], jnp.concatenate([cs[1], cs[2]], axis=0)) * (2.0 * scale)
-            late.start([last - jnp.concatenate([p1, p0], axis=1)])
-            post(0, step + 1, product(x_next, s_mat[...], dot))
+            last = last + inner(x_next, jnp.concatenate([none, c_next], axis=0))
+            late.start([last * (2.0 * scale)])
+            post(0, step + 1, listed)
         if step + 1 < STEPS:
             post(1, step + 1, product(c_next, t_mat[...], dot_nt) * list_weight)
         if step == 0:
-            p0 = dot_nt(x_ref[...], ct_ref[...]) * scale
-            p1 = dot_nt(xs[1].astype(BF16), ct_ref[...]) * scale
-            p2 = inner(xs[1], cs[1]) * (2.0 * scale) - p0
-            early.start([jnp.concatenate([p0, p1], axis=1), halves(p2)])
+            heard(2)
+            spread(3)
+            p0 = dot_nt(x_ref[...], ct_ref[...])
+            p1 = dot_nt(xs[1].astype(BF16), ct_ref[...])
+            p2 = 2.0 * inner(xs[1], cs[1]) - p0
+            half_early = 0.5 * jnp.concatenate([p1, p0], axis=1)
+            early.start([scale * jnp.concatenate([p0, p1], axis=1), scale * halves(p2)])
         if step == 1:
+            heard(3)
             early.across()
         if step < STEPS - 1:
             term_out, term_mg = out_term(step), mg_term(step)
@@ -412,6 +431,7 @@
                 pltpu.VMEM((STENCIL, PIX), F32),
                 pltpu.VMEM((PEERS, HALO), jnp.int32),
                 dma((6,)),
+                pltpu.SemaphoreType.REGULAR((4,)),
                 pltpu.VMEM((PIX, PIX), BF16),
                 pltpu.VMEM((PIX, PIX), BF16),
                 pltpu.VMEM((PIX, LISTED), BF16),

time: 45.6 us -> 44.7 us (0.980)
  Pallas kernels: 44.8 us -> 43.9 us
    pallas_call x1, Pallas kernels: 44.1 us -> 43.2 us  [local(): pl.pallas_call(body, out_shape=(pltpu.VMEM((CH, PIX), BF16), pltpu.VMEM((...]
where the time goes in v4:
time: 44.7 us; the launch traced here: 44.6 us
  Pallas kernels  43.9 us (98%)
  between operations  0.64 us (1%)
    pallas_call x1, Pallas kernels, local(): pl.pallas_call(body, out_shape=(pltpu.VMEM((CH, PIX), BF16), pltpu.VMEM((...  43.2 us

profile of v4, /device:TPU:1, one launch (start us, length us, event | category | flops | bytes accessed | tf_op | source)
XLA Modules:
  0.0 44.6 jit_solution(2878384998762267234)
XLA Ops:
  0.6 43.2 %shard_map.85 = (bf16[64,256]{1,0:T(8,128)(2,1)S(1)}, bf16[64,256]{1,0:T(8,128)(2,1)S(1)}, f32[5,64,64]{2,1,0:T(8,128)S(1)}) custom-call(bf16[64,256]{1,0:T(8,128)(2,1)} %refs_0_.1, bf16[320,64]{1,0:T(8,128)(2,1)} %bitcast.1, bf16[64,256]{1,0:T(8,128)(2,1)} %refs_2_.1, s32[9,256]{1,0:T(8,128)} %refs_3_.1, f32[9,256]{1,0:T(8,128)} %refs_4_.1, s32[8,64]{1,0:T(8,128)} %refs_5_.1), custom_call_target="tpu_custom_call" | custom-call | tf_op jit(solution)/shard_map/pallas_call | solution.py:417
  43.9 0.7 %shard_map.86 = (bf16[64,256]{1,0:T(8,128)(2,1)}, bf16[64,256]{1,0:T(8,128)(2,1)}, f32[5,64,64]{2,1,0:T(8,128)}) custom-call(bf16[64,256]{1,0:T(8,128)(2,1)S(1)} %get-tuple-element.6.out_ref, bf16[64,256]{1,0:T(8,128)(2,1)S(1)} %get-tuple-element.7.mg_ref, f32[5,64,64]{2,1,0:T(8,128)S(1)} %get-tuple-element.8.wg_ref), custom_call_target="tpu_custom_call" | custom-call | tf_op jit(solution)/shard_map/pallas_call | solution.py:467

commit v5 on v4

--- a/solution.py
+++ b/solution.py
@@ -323,8 +323,8 @@
         if step == 2:
             late.across()
         if step == 3:
+            early.back()
             late.back()
-            early.back()
         if step == 0:
             heard(0)
             spread(1)

time: 44.7 us -> 44.1 us (0.987)
  Pallas kernels: 43.9 us -> 43.3 us
    pallas_call x1, Pallas kernels: 43.2 us -> 42.6 us  [local(): pl.pallas_call(body, out_shape=(pltpu.VMEM((CH, PIX), BF16), pltpu.VMEM((...]
where the time goes in v5:
time: 44.1 us; the launch traced here: 44 us
  Pallas kernels  43.3 us (98%)
  between operations  0.64 us (1%)
    pallas_call x1, Pallas kernels, local(): pl.pallas_call(body, out_shape=(pltpu.VMEM((CH, PIX), BF16), pltpu.VMEM((...  42.6 us

profile of v5, /device:TPU:1, one launch (start us, length us, event | category | flops | bytes accessed | tf_op | source)
XLA Modules:
  0.0 44.0 jit_solution(13395873892203534965)
XLA Ops:
  0.6 42.6 %shard_map.85 = (bf16[64,256]{1,0:T(8,128)(2,1)S(1)}, bf16[64,256]{1,0:T(8,128)(2,1)S(1)}, f32[5,64,64]{2,1,0:T(8,128)S(1)}) custom-call(bf16[64,256]{1,0:T(8,128)(2,1)} %refs_0_.1, bf16[320,64]{1,0:T(8,128)(2,1)} %bitcast.1, bf16[64,256]{1,0:T(8,128)(2,1)} %refs_2_.1, s32[9,256]{1,0:T(8,128)} %refs_3_.1, f32[9,256]{1,0:T(8,128)} %refs_4_.1, s32[8,64]{1,0:T(8,128)} %refs_5_.1), custom_call_target="tpu_custom_call" | custom-call | tf_op jit(solution)/shard_map/pallas_call | solution.py:417
  43.3 0.7 %shard_map.86 = (bf16[64,256]{1,0:T(8,128)(2,1)}, bf16[64,256]{1,0:T(8,128)(2,1)}, f32[5,64,64]{2,1,0:T(8,128)}) custom-call(bf16[64,256]{1,0:T(8,128)(2,1)S(1)} %get-tuple-element.6.out_ref, bf16[64,256]{1,0:T(8,128)(2,1)S(1)} %get-tuple-element.7.mg_ref, f32[5,64,64]{2,1,0:T(8,128)S(1)} %get-tuple-element.8.wg_ref), custom_call_target="tpu_custom_call" | custom-call | tf_op jit(solution)/shard_map/pallas_call | solution.py:467

commit v6 on v5

--- a/solution.py
+++ b/solution.py
@@ -12,6 +12,8 @@
 PIX = 256
 HALO = 64
 ROW = 16
+QUAD, Y_SIZE, Z_SIZE, PLANE = 4, 4, 8, 128
+PLACES = 16
 PEERS = 8
 STENCIL = 9
 STEPS = KTERMS - 1
@@ -84,15 +86,25 @@
     *sum_refs,
 ):
     me = lax.axis_index("pix")
-    rows = count // ROW
-    my_row, my_column = me // ROW, me % ROW
+    blocks = count // PLACES
+    x_at, z_at, y_at, quad_at = me // PLANE, me // ROW % Z_SIZE, me // QUAD % Y_SIZE, me % QUAD
+    my_place, my_block = x_at * QUAD + quad_at, z_at * Y_SIZE + y_at
     peers = [(me + OFFSETS[o] + count) % count for o in ORDER]
 
-    def in_row(step):
-        return my_row * ROW + (my_column + step) % ROW
-
-    def in_column(step):
-        return (my_row + step) % rows * ROW + my_column
+    def device_at(place, block):
+        return place // QUAD * PLANE + block // Y_SIZE * ROW + block % Y_SIZE * QUAD + place % QUAD
+
+    def in_block(step):
+        return device_at((my_place + step) % PLACES, my_block)
+
+    def in_place(step):
+        return device_at(my_place, (my_block + step) % blocks)
+
+    def along_z(step):
+        return me + ((z_at + step) % Z_SIZE - z_at) * ROW
+
+    def along_y(step):
+        return me + ((y_at + step) % Y_SIZE - y_at) * QUAD
 
     barrier = pltpu.get_barrier_semaphore()
 
@@ -101,8 +113,6 @@
 
     for peer in peers:
         greet(peer)
-    for step in (1, ROW - 1):
-        greet(in_row(step))
 
     loads = [
         pltpu.make_async_copy(src, dst, load_sem.at[i])
@@ -120,16 +130,25 @@
     for load in loads:
         load.start()
 
+    for ring, size in ((along_z, Z_SIZE), (along_y, Y_SIZE)):
+        greet(ring(1))
+        greet(ring(size - 1))
+
+    @pl.loop(1, PLACES)
+    def _(step):
+        greet(in_block(step))
+
+    spreads = ((along_z, 1, Z_SIZE), (along_z, 2, Z_SIZE), (along_y, 1, Y_SIZE), (along_y, 1, Y_SIZE))
+
     def spread(k):
-        for ring, size in ((in_row, ROW), (in_column, rows)):
-            if 4 * 2**k <= size:
-                for other in (2**k, size - 2**k):
-                    pl.semaphore_signal(
-                        known.at[k], inc=1, device_id=(ring(other),), device_id_type=MESH
-                    )
+        ring, reach, size = spreads[k]
+        for other in (reach, size - reach):
+            pl.semaphore_signal(
+                known.at[k], inc=1, device_id=(ring(other),), device_id_type=MESH
+            )
 
     def heard(k):
-        pl.semaphore_wait(known.at[k], sum(2 for size in (ROW, rows) if 4 * 2**k <= size))
+        pl.semaphore_wait(known.at[k], 2)
 
     lane_low = lax.broadcasted_iota(jnp.int32, (CH // 2, 128), 1) < HALO
 
@@ -204,7 +223,7 @@
     loads[4].wait()
     cs = [ct_ref[...].astype(F32)]
     post(1, 0, dot_nt(ct_ref[...], t_mat[...]) * list_weight, start=False)
-    pl.semaphore_wait(barrier, PEERS + 2)
+    pl.semaphore_wait(barrier, PEERS + 4 + PLACES - 1)
     for chain in range(2):
         for place in range(PEERS):
             halo_copy(chain, 0, place).start()
@@ -242,7 +261,7 @@
     class Batch:
         def __init__(self, which):
             self.which = which
-            self.sums, self.row_in, self.part, self.column_in, self.total = sum_refs[
+            self.sums, self.block_in, self.part, self.place_in, self.total = sum_refs[
                 5 * which : 5 * which + 5
             ]
 
@@ -257,51 +276,49 @@
             )
 
         def all_of(self, stage):
-            ref = (self.row_in, self.column_in, self.total)[stage]
-            ref = ref.at[pl.ds(0, (ROW, rows, ROW)[stage] - 1)]
+            ref = (self.block_in, self.place_in, self.total)[stage]
+            ref = ref.at[pl.ds(0, (PLACES, blocks, PLACES)[stage] - 1)]
             return self.copy(stage, ref, ref, peers[0])
 
         def start(self, blocks):
             at = 0
             for block in blocks:
-                n = block.shape[0] // ROW
-                for i in range(ROW):
+                n = block.shape[0] // PLACES
+                for i in range(PLACES):
                     self.sums[i, at : at + n, :] = block[n * i : n * i + n]
                 at += n
 
-            @pl.loop(1, ROW)
+            @pl.loop(1, PLACES)
             def _(i):
-                other = (my_column + i) % ROW
-                self.copy(
-                    0, self.sums.at[other], self.row_in.at[my_column], my_row * ROW + other
-                ).start()
-
-            self.row_in[my_column] = self.sums[my_column]
+                mine = self.sums.at[(my_place + i) % PLACES]
+                self.copy(0, mine, self.block_in.at[my_place], in_block(i)).start()
+
+            self.block_in[my_place] = self.sums[my_place]
 
         def across(self):
             self.all_of(0).wait_recv()
-            piece = self.row_in[0]
-            for i in range(1, ROW):
-                piece = piece + self.row_in[i]
+            piece = self.block_in[0]
+            for i in range(1, PLACES):
+                piece = piece + self.block_in[i]
             self.part[...] = piece
 
-            @pl.loop(1, rows)
+            @pl.loop(1, blocks)
             def _(i):
-                self.copy(1, self.part, self.column_in.at[my_row], in_column(i)).start()
-
-            self.column_in[my_row] = piece
+                self.copy(1, self.part, self.place_in.at[my_block], in_place(i)).start()
+
+            self.place_in[my_block] = piece
 
         def back(self):
             self.all_of(1).wait_recv()
-            piece = self.column_in[0]
-            for i in range(1, rows):
-                piece = piece + self.column_in[i]
-            self.total[my_column] = piece
-
-            @pl.loop(1, ROW)
+            piece = self.place_in[0]
+            for i in range(1, blocks):
+                piece = piece + self.place_in[i]
+            self.total[my_place] = piece
+
+            @pl.loop(1, PLACES)
             def _(i):
-                mine = self.total.at[my_column]
-                self.copy(2, mine, mine, in_row(i)).start()
+                mine = self.total.at[my_place]
+                self.copy(2, mine, mine, in_block(i)).start()
 
         def arrive(self):
             self.all_of(2).wait_recv()
@@ -352,13 +369,13 @@
         if step + 1 < STEPS:
             post(1, step + 1, product(c_next, t_mat[...], dot_nt) * list_weight)
         if step == 0:
-            heard(2)
-            spread(3)
             p0 = dot_nt(x_ref[...], ct_ref[...])
             p1 = dot_nt(xs[1].astype(BF16), ct_ref[...])
             p2 = 2.0 * inner(xs[1], cs[1]) - p0
             half_early = 0.5 * jnp.concatenate([p1, p0], axis=1)
             early.start([scale * jnp.concatenate([p0, p1], axis=1), scale * halves(p2)])
+            heard(2)
+            spread(3)
         if step == 1:
             heard(3)
             early.across()
@@ -375,7 +392,7 @@
     early.arrive()
 
     def rows_of(batch, lower, upper):
-        return jnp.concatenate([batch.total[i, lower:upper, :] for i in range(ROW)], axis=0)
+        return jnp.concatenate([batch.total[i, lower:upper, :] for i in range(PLACES)], axis=0)
 
     first = rows_of(early, 0, 4)
     third = rows_of(early, 4, 6)
@@ -407,7 +424,7 @@
 
 def solution(mesh):
     count = mesh.shape["pix"]
-    rows = count // ROW
+    blocks = count // PLACES
     dma = pltpu.SemaphoreType.DMA
 
     def local(input_maps, cheb_weights, cotangent, neighbours, lap_weights, send_rows):
@@ -445,7 +462,7 @@
                 *[
                     pltpu.VMEM(lead + (share, 128), F32)
                     for share in SHARES
-                    for lead in ((ROW,), (ROW,), (), (rows,), (ROW,))
+                    for lead in ((PLACES,), (PLACES,), (), (blocks,), (PLACES,))
                 ],
             ],
             compiler_params=pltpu.CompilerParams(

time: 44.1 us -> 43.5 us (0.986)
  Pallas kernels: 43.3 us -> 42.8 us
    pallas_call x1, Pallas kernels: 42.6 us -> 42 us  [local(): pl.pallas_call(body, out_shape=(pltpu.VMEM((CH, PIX), BF16), pltpu.VMEM((...]
where the time goes in v6:
time: 43.5 us; the launch traced here: 43.4 us
  Pallas kernels  42.8 us (98%)
  between operations  0.64 us (1%)
    pallas_call x1, Pallas kernels, local(): pl.pallas_call(body, out_shape=(pltpu.VMEM((CH, PIX), BF16), pltpu.VMEM((...  42 us

profile of v6, /device:TPU:1, one launch (start us, length us, event | category | flops | bytes accessed | tf_op | source)
XLA Modules:
  0.0 43.4 jit_solution(12066854996047700787)
XLA Ops:
  0.6 42.0 %shard_map.85 = (bf16[64,256]{1,0:T(8,128)(2,1)S(1)}, bf16[64,256]{1,0:T(8,128)(2,1)S(1)}, f32[5,64,64]{2,1,0:T(8,128)S(1)}) custom-call(bf16[64,256]{1,0:T(8,128)(2,1)} %refs_0_.1, bf16[320,64]{1,0:T(8,128)(2,1)} %bitcast.1, bf16[64,256]{1,0:T(8,128)(2,1)} %refs_2_.1, s32[9,256]{1,0:T(8,128)} %refs_3_.1, f32[9,256]{1,0:T(8,128)} %refs_4_.1, s32[8,64]{1,0:T(8,128)} %refs_5_.1), custom_call_target="tpu_custom_call" | custom-call | tf_op jit(solution)/shard_map/pallas_call | solution.py:434
  42.7 0.7 %shard_map.86 = (bf16[64,256]{1,0:T(8,128)(2,1)}, bf16[64,256]{1,0:T(8,128)(2,1)}, f32[5,64,64]{2,1,0:T(8,128)}) custom-call(bf16[64,256]{1,0:T(8,128)(2,1)S(1)} %get-tuple-element.6.out_ref, bf16[64,256]{1,0:T(8,128)(2,1)S(1)} %get-tuple-element.7.mg_ref, f32[5,64,64]{2,1,0:T(8,128)S(1)} %get-tuple-element.8.wg_ref), custom_call_target="tpu_custom_call" | custom-call | tf_op jit(solution)/shard_map/pallas_call | solution.py:484

commit v7 on v6

--- a/solution.py
+++ b/solution.py
@@ -111,9 +111,6 @@
     def greet(device):
         pl.semaphore_signal(barrier, inc=1, device_id=(device,), device_id_type=MESH)
 
-    for peer in peers:
-        greet(peer)
-
     loads = [
         pltpu.make_async_copy(src, dst, load_sem.at[i])
         for i, (src, dst) in enumerate(
@@ -129,6 +126,9 @@
     ]
     for load in loads:
         load.start()
+
+    for peer in peers:
+        greet(peer)
 
     for ring, size in ((along_z, Z_SIZE), (along_y, Y_SIZE)):
         greet(ring(1))
@@ -288,8 +288,7 @@
                     self.sums[i, at : at + n, :] = block[n * i : n * i + n]
                 at += n
 
-            @pl.loop(1, PLACES)
-            def _(i):
+            for i in range(1, PLACES):
                 mine = self.sums.at[(my_place + i) % PLACES]
                 self.copy(0, mine, self.block_in.at[my_place], in_block(i)).start()
 
@@ -302,8 +301,7 @@
                 piece = piece + self.block_in[i]
             self.part[...] = piece
 
-            @pl.loop(1, blocks)
-            def _(i):
+            for i in range(1, blocks):
                 self.copy(1, self.part, self.place_in.at[my_block], in_place(i)).start()
 
             self.place_in[my_block] = piece
@@ -315,8 +313,7 @@
                 piece = piece + self.place_in[i]
             self.total[my_place] = piece
 
-            @pl.loop(1, PLACES)
-            def _(i):
+            for i in range(1, PLACES):
                 mine = self.total.at[my_place]
                 self.copy(2, mine, mine, in_block(i)).start()
 

time: 43.5 us -> 43.4 us (level)
  no operation moved by 1% of the time
where the time goes in v7:
time: 43.4 us; the launch traced here: 43.2 us
  Pallas kernels  42.6 us (98%)
  between operations  0.64 us (1%)
    pallas_call x1, Pallas kernels, local(): pl.pallas_call(body, out_shape=(pltpu.VMEM((CH, PIX), BF16), pltpu.VMEM((...  41.9 us

profile of v7, /device:TPU:1, one launch (start us, length us, event | category | flops | bytes accessed | tf_op | source)
XLA Modules:
  0.0 43.2 jit_solution(5856593917536995049)
XLA Ops:
  0.6 41.9 %shard_map.85 = (bf16[64,256]{1,0:T(8,128)(2,1)S(1)}, bf16[64,256]{1,0:T(8,128)(2,1)S(1)}, f32[5,64,64]{2,1,0:T(8,128)S(1)}) custom-call(bf16[64,256]{1,0:T(8,128)(2,1)} %refs_0_.1, bf16[320,64]{1,0:T(8,128)(2,1)} %bitcast.1, bf16[64,256]{1,0:T(8,128)(2,1)} %refs_2_.1, s32[9,256]{1,0:T(8,128)} %refs_3_.1, f32[9,256]{1,0:T(8,128)} %refs_4_.1, s32[8,64]{1,0:T(8,128)} %refs_5_.1), custom_call_target="tpu_custom_call" | custom-call | tf_op jit(solution)/shard_map/pallas_call | solution.py:431
  42.5 0.7 %shard_map.86 = (bf16[64,256]{1,0:T(8,128)(2,1)}, bf16[64,256]{1,0:T(8,128)(2,1)}, f32[5,64,64]{2,1,0:T(8,128)}) custom-call(bf16[64,256]{1,0:T(8,128)(2,1)S(1)} %get-tuple-element.6.out_ref, bf16[64,256]{1,0:T(8,128)(2,1)S(1)} %get-tuple-element.7.mg_ref, f32[5,64,64]{2,1,0:T(8,128)S(1)} %get-tuple-element.8.wg_ref), custom_call_target="tpu_custom_call" | custom-call | tf_op jit(solution)/shard_map/pallas_call | solution.py:481

commit v8 on v7

--- a/solution.py
+++ b/solution.py
@@ -48,6 +48,13 @@
     both = times(jnp.concatenate([high, low], axis=0), matrix)
     rows = value.shape[0]
     return both[:rows] + both[rows:]
+
+
+def added(terms):
+    while len(terms) > 1:
+        half = len(terms) // 2
+        terms = [a + b for a, b in zip(terms[:half], terms[half:])]
+    return terms[0]
 
 
 def turned(value):
@@ -134,9 +141,9 @@
         greet(ring(1))
         greet(ring(size - 1))
 
-    @pl.loop(1, PLACES)
-    def _(step):
-        greet(in_block(step))
+    others = [((my_place + i) % PLACES, in_block(i)) for i in range(1, PLACES)]
+    for _, device in others:
+        greet(device)
 
     spreads = ((along_z, 1, Z_SIZE), (along_z, 2, Z_SIZE), (along_y, 1, Y_SIZE), (along_y, 1, Y_SIZE))
 
@@ -227,6 +234,7 @@
     for chain in range(2):
         for place in range(PEERS):
             halo_copy(chain, 0, place).start()
+    like_placed = [in_place(i) for i in range(1, blocks)]
     spread(0)
 
     for base in range(0, PIX, 32):
@@ -288,34 +296,30 @@
                     self.sums[i, at : at + n, :] = block[n * i : n * i + n]
                 at += n
 
-            for i in range(1, PLACES):
-                mine = self.sums.at[(my_place + i) % PLACES]
-                self.copy(0, mine, self.block_in.at[my_place], in_block(i)).start()
+            for place, device in others:
+                mine = self.sums.at[place]
+                self.copy(0, mine, self.block_in.at[my_place], device).start()
 
             self.block_in[my_place] = self.sums[my_place]
 
         def across(self):
             self.all_of(0).wait_recv()
-            piece = self.block_in[0]
-            for i in range(1, PLACES):
-                piece = piece + self.block_in[i]
+            piece = added([self.block_in[i] for i in range(PLACES)])
             self.part[...] = piece
 
-            for i in range(1, blocks):
-                self.copy(1, self.part, self.place_in.at[my_block], in_place(i)).start()
+            for device in like_placed:
+                self.copy(1, self.part, self.place_in.at[my_block], device).start()
 
             self.place_in[my_block] = piece
 
         def back(self):
             self.all_of(1).wait_recv()
-            piece = self.place_in[0]
-            for i in range(1, blocks):
-                piece = piece + self.place_in[i]
+            piece = added([self.place_in[i] for i in range(blocks)])
             self.total[my_place] = piece
 
-            for i in range(1, PLACES):
-                mine = self.total.at[my_place]
-                self.copy(2, mine, mine, in_block(i)).start()
+            mine = self.total.at[my_place]
+            for _, device in others:
+                self.copy(2, mine, mine, device).start()
 
         def arrive(self):
             self.all_of(2).wait_recv()

time: 43.4 us -> 43.3 us (level)
  no operation moved by 1% of the time
where the time goes in v8:
time: 43.3 us; the launch traced here: 43.2 us
  Pallas kernels  42.5 us (98%)
  between operations  0.64 us (1%)
    pallas_call x1, Pallas kernels, local(): pl.pallas_call(body, out_shape=(pltpu.VMEM((CH, PIX), BF16), pltpu.VMEM((...  41.8 us

profile of v8, /device:TPU:1, one launch (start us, length us, event | category | flops | bytes accessed | tf_op | source)
XLA Modules:
  0.0 43.2 jit_solution(2177358505245785169)
XLA Ops:
  0.6 41.8 %shard_map.85 = (bf16[64,256]{1,0:T(8,128)(2,1)S(1)}, bf16[64,256]{1,0:T(8,128)(2,1)S(1)}, f32[5,64,64]{2,1,0:T(8,128)S(1)}) custom-call(bf16[64,256]{1,0:T(8,128)(2,1)} %refs_0_.1, bf16[320,64]{1,0:T(8,128)(2,1)} %bitcast.1, bf16[64,256]{1,0:T(8,128)(2,1)} %refs_2_.1, s32[9,256]{1,0:T(8,128)} %refs_3_.1, f32[9,256]{1,0:T(8,128)} %refs_4_.1, s32[8,64]{1,0:T(8,128)} %refs_5_.1), custom_call_target="tpu_custom_call" | custom-call | tf_op jit(solution)/shard_map/pallas_call | solution.py:435
  42.4 0.7 %shard_map.86 = (bf16[64,256]{1,0:T(8,128)(2,1)}, bf16[64,256]{1,0:T(8,128)(2,1)}, f32[5,64,64]{2,1,0:T(8,128)}) custom-call(bf16[64,256]{1,0:T(8,128)(2,1)S(1)} %get-tuple-element.6.out_ref, bf16[64,256]{1,0:T(8,128)(2,1)S(1)} %get-tuple-element.7.mg_ref, f32[5,64,64]{2,1,0:T(8,128)S(1)} %get-tuple-element.8.wg_ref), custom_call_target="tpu_custom_call" | custom-call | tf_op jit(solution)/shard_map/pallas_call | solution.py:485
